TPU v7x, 128 devices: a whole 4x4x4 slice. The times are simulated.
128 devices in a mesh: gx: 8 (over z, core), gy: 16 (over x, y).
Axes of the slice: x: 4, y: 4, z: 4, core: 2. Of those that a mesh axis runs over, the one named last changes fastest.
Arguments:
- leaf_up: float32 [192, 256, 456], P('gx', 'gy'), may hold values from -6 to 6
- parent_in: float32 [96, 128, 456], P('gx', 'gy'), may hold values from -6 to 6
- leaf_lists: int32 [192, 256, 40], P('gx', 'gy'), may hold values from 0 to 1, as said below
- parent_lists: int32 [96, 128, 40], P('gx', 'gy'), may hold values from 0 to 1, as said below
- up_transfer: float32 [4, 456, 456], replicated, may hold values from -0.125 to 0.125
- down_transfer: float32 [4, 456, 456], replicated, may hold values from -0.25 to 0.25
- check_inverse: float32 [456, 456], replicated, may hold values from -0.25 to 0.25
Outputs:
- leaf_down: float32 [192, 256, 456], P('gx', 'gy')
- parent_up: float32 [96, 128, 456], P('gx', 'gy')
Inputs may be any that keep to these rules, and one draw needn't show every extreme that they name: `leaf_lists`: A flag is 1 only where the box at that offset lies in the grid, its parent touches or equals the box's parent, and it holds surface points. `parent_lists`: A flag is 1 only where the parent at that offset lies in the grid, its parent touches or equals the box's parent, and it holds surface points.
All inputs are finite; a program needn't handle non-finite values.
Results may differ from a plain program's by a relative error of at most 0.0001.
Values sent between devices are 32-bit elements; how exact they have to be, the bound alone decides.
A program may use at most 64 MiB of HBM per device.

v0:
```python
import math

import jax
import jax.numpy as jnp
import numpy as np
from jax import lax
from jax.sharding import PartitionSpec as P

ORDER = 6


stokes_scale = 1.0 / (8.0 * math.pi)


def extended(shard, sides, width):
    for axis, dim in sides:
        peers, length = (lax.axis_size(axis), shard.shape[dim])
        up = [(i, (i + 1) % peers) for i in range(peers - 1)]
        down = [(j, i) for i, j in up]
        last = lax.slice_in_dim(shard, length - width, length, axis=dim)
        initial = lax.slice_in_dim(shard, 0, width, axis=dim)
        before = lax.ppermute(last, axis, up)
        after = lax.ppermute(initial, axis, down)
        shard = jnp.concatenate([before, shard, after], axis=dim)
    return shard


def offset_table():
    chosen = [(a, b) for a in range(-3, 4) for b in range(-3, 4) if max(abs(a), abs(b)) >= 2]
    return np.array(chosen, dtype=np.int32)


def surface_points():
    grid_line = np.linspace(-1.0, 1.0, ORDER)
    points = []
    for i in range(ORDER):
        for j in range(ORDER):
            for k in range(ORDER):
                if min(i, j, k) == 0 or max(i, j, k) == ORDER - 1:
                    points.append((grid_line[i], grid_line[j], grid_line[k]))
    return np.array(points, dtype=np.float32).T


def kernel_matrix(shift_row, shift_col):
    surface = surface_points()
    spacing = 0.525 * (surface[:, :, None] - surface[:, None, :])
    components = (
        jnp.asarray(spacing[0]) - shift_row,
        jnp.asarray(spacing[1]) - shift_col,
        jnp.asarray(spacing[2]) + 0.0 * shift_row,
    )
    squared = (
        components[0] * components[0]
        + components[1] * components[1]
        + components[2] * components[2]
    )
    inverse = 1.0 / jnp.sqrt(squared)
    cubed = inverse * inverse * inverse
    blocks = []
    for a in range(3):
        line_blocks = []
        for b in range(3):
            entry = components[a] * components[b] * cubed
            if a == b:
                entry = entry + inverse
            line_blocks.append(entry * stokes_scale)
        blocks.append(jnp.concatenate(line_blocks, axis=1))
    return jnp.concatenate(blocks, axis=0)


def interact(padded, lists, row_count, col_count):
    features = padded.shape[2]
    offsets = jnp.asarray(offset_table()).reshape(10, 4, 2)
    picks = jnp.arange(40, dtype=jnp.int32).reshape(10, 4)

    def advance(running, cluster):
        pairs_now, picks_now = cluster
        sources = []
        matrices = []
        for member in range(4):
            offset_pair = pairs_now[member]
            source = lax.dynamic_slice(
                padded,
                (offset_pair[0] + 3, offset_pair[1] + 3, jnp.int32(0)),
                (row_count, col_count, features),
            )
            weight = lax.dynamic_slice_in_dim(lists, picks_now[member], 1, 2).astype(jnp.float32)
            sources.append((source * weight).reshape(row_count * col_count, features))
            matrices.append(
                kernel_matrix(
                    offset_pair[0].astype(jnp.float32), offset_pair[1].astype(jnp.float32)
                )
            )
        stacked_source = jnp.concatenate(sources, axis=1)
        stacked_matrix = jnp.concatenate(matrices, axis=1)
        product = lax.dot_general(
            stacked_source,
            stacked_matrix,
            (((1,), (1,)), ((), ())),
            precision=lax.Precision.HIGHEST,
            preferred_element_type=jnp.float32,
        )
        return (running + product, None)

    start = jnp.zeros((row_count * col_count, features), jnp.float32)
    running, _ = lax.scan(advance, start, (offsets, picks))
    return running


def gather_children(leaf_values, up_transfer):
    row_count, col_count, features = leaf_values.shape
    grouped = leaf_values.reshape(row_count // 2, 2, col_count // 2, 2, features)
    operators = up_transfer.reshape(2, 2, features, features)
    return jnp.einsum("acbdk,cdjk->abj", grouped, operators, precision=lax.Precision.HIGHEST)


def spread_children(parent_values, down_transfer):
    row_count, col_count, features = parent_values.shape
    operators = down_transfer.reshape(2, 2, features, features)
    spread = jnp.einsum(
        "abk,cdjk->acbdj", parent_values, operators, precision=lax.Precision.HIGHEST
    )
    return spread.reshape(2 * row_count, 2 * col_count, features)


def apply_inverse(check_values, check_inverse):
    return lax.dot_general(
        check_values,
        check_inverse,
        (((1,), (1,)), ((), ())),
        precision=lax.Precision.HIGHEST,
        preferred_element_type=jnp.float32,
    )


def local(leaf_up, parent_in, leaf_lists, parent_lists, up_transfer, down_transfer, check_inverse):
    leaf_rows_here, leaf_cols_here, features = leaf_up.shape
    parent_rows_here = leaf_rows_here // 2
    parent_cols_here = leaf_cols_here // 2
    parent_up = gather_children(leaf_up, up_transfer)
    parent_near = extended(parent_up, (("gx", 0), ("gy", 1)), 3)
    parent_check = interact(parent_near, parent_lists, parent_rows_here, parent_cols_here)
    parent_local = parent_in + apply_inverse(parent_check, check_inverse).reshape(
        parent_rows_here, parent_cols_here, features
    )
    leaf_near = extended(leaf_up, (("gx", 0), ("gy", 1)), 3)
    leaf_check = interact(leaf_near, leaf_lists, leaf_rows_here, leaf_cols_here).reshape(
        leaf_rows_here, leaf_cols_here, features
    )
    leaf_check = leaf_check + spread_children(parent_local, down_transfer)
    leaf_down = apply_inverse(
        leaf_check.reshape(leaf_rows_here * leaf_cols_here, features), check_inverse
    )
    return (leaf_down.reshape(leaf_rows_here, leaf_cols_here, features), parent_up)


def solution(mesh):
    placed = (
        P("gx", "gy", None),
        P("gx", "gy", None),
        P("gx", "gy", None),
        P("gx", "gy", None),
        P(),
        P(),
        P(),
    )
    return jax.shard_map(
        local,
        mesh=mesh,
        in_specs=placed,
        out_specs=(P("gx", "gy", None), P("gx", "gy", None)),
        check_vma=False,
    )
```

profile of v0, /device:TPU:7, one launch (start us, length us, event | category | flops | bytes accessed | tf_op | source)
XLA Modules:
  0.0 954.8 jit_solution(4636367402858113952)
XLA Ops:
  9.4 5.5 convolution_bitcast_fusion.2
  22.7 4.9 collective-permute-start.7
  30.7 5.5 collective-permute-start.3
  38.5 397.8 %while.33 = (s32[]{:T(128)}, f32[96,456]{1,0:T(8,128)}, s32[10,4,2]{0,2,1:T(2,128)S(1)}, f32[18,14,456]{2,1,0:T(8,128)S(1)}, s32[10,4]{0,1:T(4,128)S(1)}, /*inde...) while((s32[]{:T(128)}, f32[96,456]{1,0:T(8,128)}, ...), condition=%wide.region_3.4_spmd.clone.clone.clone, body=%wide.region_2.3_spmd.sunk.clone.clone.clone.sunk | while | flops 967673792 | bytes 26668512 | solution.py:106
  72.2 6.0 convolution_add_fusion.5
  112.0 6.0 convolution_add_fusion.5
  151.8 6.0 convolution_add_fusion.5
  191.5 6.0 convolution_add_fusion.5
  231.3 6.0 convolution_add_fusion.5
  271.1 6.0 convolution_add_fusion.5
  310.9 6.0 convolution_add_fusion.5
  350.7 6.0 convolution_add_fusion.5
  390.5 6.0 convolution_add_fusion.5
  430.2 6.0 convolution_add_fusion.5
  438.3 5.6 convolution_bitcast_fusion
  447.6 502.3 %while.32 = (s32[]{:T(128)}, f32[384,456]{0,1:T(8,128)}, s32[10,4,2]{0,2,1:T(2,128)S(1)}, f32[30,22,456]{2,1,0:T(8,128)S(1)}, s32[10,4]{0,1:T(4,128)S(1)}, /*ind...) while((s32[]{:T(128)}, f32[384,456]{0,1:T(8,128)}, ...), condition=%wide.region_1.2_spmd.clone.clone.clone, body=%wide.region_0.1_spmd.sunk.clone.clone.clone.sunk | while | flops 3842970112 | bytes 33449788 | solution.py:106
  484.0 4.8 concatenate.417
  488.8 9.1 convolution_add_fusion.4
  534.1 4.8 concatenate.417
  538.9 9.2 convolution_add_fusion.4
  584.3 4.8 concatenate.417
  589.1 9.2 convolution_add_fusion.4
  639.3 9.2 convolution_add_fusion.4
  684.7 4.8 concatenate.417
  689.5 9.2 convolution_add_fusion.4
  739.7 9.2 convolution_add_fusion.4
  790.0 9.2 convolution_add_fusion.4
  835.4 4.8 concatenate.417
  840.2 9.2 convolution_add_fusion.4
  885.6 4.8 concatenate.417
  890.4 9.2 convolution_add_fusion.4
  940.6 9.2 convolution_add_fusion.4
  (392 shorter events, 297.2 us)
Async XLA Ops:
  0.6 435.7 %copy-start = (f32[456,456]{1,0:T(8,128)S(1)}, f32[456,456]{1,0:T(8,128)}, u32[]{:S(2)}) copy-start(f32[456,456]{1,0:T(8,128)} %param.43) | copy-start | bytes 2495236
  1.7 27.9 %collective-permute-start = (f32[3,16,456]{2,1,0:T(8,128)S(1)}, f32[3,16,456]{2,1,0:T(8,128)S(1)}, u32[]{:S(2)}, u32[]{:S(2)}) collective-permute-start(f32[3,16,456]{2,1,0:T(8,128)S(1)} %get-tuple-element.875), channel_id=1, source_target_pairs={{0,16},{16,32},{32,48},{48,64},{64,80},{80,96},{96,112},{1,17},{17... | collective-permute-start | bytes 262664 | tf_op jit(solution)/shard_map/ppermute | solution.py:22
  5.8 23.9 %collective-permute-start.1 = (f32[3,16,456]{2,1,0:T(8,128)S(1)}, f32[3,16,456]{2,1,0:T(8,128)S(1)}, u32[]{:S(2)}, u32[]{:S(2)}) collective-permute-start(f32[3,16,456]{2,1,0:T(8,128)S(1)} %get-tuple-element.874), channel_id=1, source_target_pairs={{16,0},{32,16},{48,32},{64,48},{80,64},{96,80},{112,96},{17,1},{33... | collective-permute-start | bytes 262664 | tf_op jit(solution)/shard_map/ppermute | solution.py:23
  9.4 11.4 %copy-start.14 = (s32[24,16,40]{2,1,0:T(8,128)S(1)}, s32[24,16,40]{2,1,0:T(8,128)}, u32[]{:S(2)}) copy-start(s32[24,16,40]{2,1,0:T(8,128)} %param.39) | copy-start | bytes 184324
  9.4 12.4 %copy-start.15 = (s32[12,8,40]{2,1,0:T(8,128)S(1)}, s32[12,8,40]{2,1,0:T(8,128)}, u32[]{:S(2)}) copy-start(s32[12,8,40]{2,1,0:T(8,128)} %param.40) | copy-start | bytes 46084
  9.4 20.2 %copy-start.3 = (f32[24,16,456]{2,1,0:T(8,128)S(1)}, f32[24,16,456]{2,1,0:T(8,128)}, u32[]{:S(2)}) copy-start(f32[24,16,456]{2,1,0:T(8,128)} %param.37) | copy-start | bytes 2101252
  15.0 23.5 %copy-start.12 = (f32[12,8,456]{2,1,0:T(8,128)}, f32[12,8,456]{2,1,0:T(8,128)S(1)}, u32[]{:S(2)}) copy-start(f32[12,8,456]{2,1,0:T(8,128)S(1)} %convolution_bitcast_fusion.2) | copy-start | bytes 525316
  15.0 23.5 %copy-start.5 = (f32[152,152]{1,0:T(8,128)S(1)}, f32[152,152]{1,0:T(8,128)}, u32[]{:S(2)}) copy-start(f32[152,152]{1,0:T(8,128)} %constant.174.clone..sunk.22) | copy-start | bytes 277252
  15.0 23.5 %copy-start.7 = (f32[152,152]{1,0:T(8,128)S(1)}, f32[152,152]{1,0:T(8,128)}, u32[]{:S(2)}) copy-start(f32[152,152]{1,0:T(8,128)} %constant.176.clone..sunk.22) | copy-start | bytes 277252
  15.0 23.5 %copy-start.9 = (f32[152,152]{1,0:T(8,128)S(1)}, f32[152,152]{1,0:T(8,128)}, u32[]{:S(2)}) copy-start(f32[152,152]{1,0:T(8,128)} %constant.175.clone..sunk.22) | copy-start | bytes 277252
  15.0 23.5 %copy-start.13 = (s32[10,4,2]{0,2,1:T(2,128)S(1)}, s32[10,4,2]{0,2,1:T(2,128)}, u32[]{:S(2)}) copy-start(s32[10,4,2]{0,2,1:T(2,128)} %constant.179) | copy-start | bytes 964
  15.0 7.6 collective-permute-start.5
  17.1 5.5 collective-permute-start.4
  22.7 15.6 %collective-permute-start.7 = (f32[18,3,456]{2,1,0:T(4,128)S(1)}, f32[18,3,456]{2,1,0:T(4,128)S(1)}, u32[]{:S(2)}, u32[]{:S(2)}) collective-permute-start(f32[18,3,456]{2,1,0:T(4,128)S(1)} %get-tuple-element.877), channel_id=1, source_target_pairs={{1,0},{2,1},{3,2},{4,3},{5,4},{6,5},{7,6},{8,7},{9,8},{10,9},{11,1... | collective-permute-start | bytes 295496 | tf_op jit(solution)/shard_map/ppermute | solution.py:23
  27.6 10.7 %collective-permute-start.6 = (f32[18,3,456]{2,1,0:T(4,128)S(1)}, f32[18,3,456]{2,1,0:T(4,128)S(1)}, u32[]{:S(2)}, u32[]{:S(2)}) collective-permute-start(f32[18,3,456]{2,1,0:T(4,128)S(1)} %get-tuple-element.876), channel_id=1, source_target_pairs={{0,1},{1,2},{2,3},{3,4},{4,5},{5,6},{6,7},{7,8},{8,9},{9,10},{10,1... | collective-permute-start | bytes 295496 | tf_op jit(solution)/shard_map/ppermute | solution.py:22
  29.7 8.6 copy-start.11
  30.7 415.2 %collective-permute-start.3 = (f32[30,3,456]{2,1,0:T(4,128)}, f32[30,3,456]{2,1,0:T(4,128)}, u32[]{:S(2)}, u32[]{:S(2)}) collective-permute-start(f32[30,3,456]{2,1,0:T(4,128)} %get-tuple-element.873), channel_id=1, source_target_pairs={{1,0},{2,1},{3,2},{4,3},{5,4},{6,5},{7,6},{8,7},{9,8},{10,9},{11,1... | collective-permute-start | bytes 492488 | tf_op jit(solution)/shard_map/ppermute | solution.py:23
  36.2 409.8 %collective-permute-start.2 = (f32[30,3,456]{2,1,0:T(4,128)}, f32[30,3,456]{2,1,0:T(4,128)}, u32[]{:S(2)}, u32[]{:S(2)}) collective-permute-start(f32[30,3,456]{2,1,0:T(4,128)} %get-tuple-element.872), channel_id=1, source_target_pairs={{0,1},{1,2},{2,3},{3,4},{4,5},{5,6},{6,7},{7,8},{8,9},{9,10},{10,1... | collective-permute-start | bytes 492488 | tf_op jit(solution)/shard_map/ppermute | solution.py:22
  38.5 26.3 %copy-start.1 = (f32[18,14,456]{2,1,0:T(8,128)}, f32[18,14,456]{2,1,0:T(8,128)S(1)}, u32[]{:S(2)}) copy-start(f32[18,14,456]{2,1,0:T(8,128)S(1)} %get-tuple-element.1244) | copy-start | bytes 1378948 | tf_op jit(solution)/shard_map/while
  72.2 6.1 copy-start.8
  72.2 6.1 copy-start.10
  78.3 26.3 %copy-start.1 = (f32[18,14,456]{2,1,0:T(8,128)}, f32[18,14,456]{2,1,0:T(8,128)S(1)}, u32[]{:S(2)}) copy-start(f32[18,14,456]{2,1,0:T(8,128)S(1)} %get-tuple-element.1244) | copy-start | bytes 1378948 | tf_op jit(solution)/shard_map/while
  118.1 26.3 %copy-start.1 = (f32[18,14,456]{2,1,0:T(8,128)}, f32[18,14,456]{2,1,0:T(8,128)S(1)}, u32[]{:S(2)}) copy-start(f32[18,14,456]{2,1,0:T(8,128)S(1)} %get-tuple-element.1244) | copy-start | bytes 1378948 | tf_op jit(solution)/shard_map/while
  157.8 26.3 %copy-start.1 = (f32[18,14,456]{2,1,0:T(8,128)}, f32[18,14,456]{2,1,0:T(8,128)S(1)}, u32[]{:S(2)}) copy-start(f32[18,14,456]{2,1,0:T(8,128)S(1)} %get-tuple-element.1244) | copy-start | bytes 1378948 | tf_op jit(solution)/shard_map/while
  197.6 26.3 %copy-start.1 = (f32[18,14,456]{2,1,0:T(8,128)}, f32[18,14,456]{2,1,0:T(8,128)S(1)}, u32[]{:S(2)}) copy-start(f32[18,14,456]{2,1,0:T(8,128)S(1)} %get-tuple-element.1244) | copy-start | bytes 1378948 | tf_op jit(solution)/shard_map/while
  237.4 26.3 %copy-start.1 = (f32[18,14,456]{2,1,0:T(8,128)}, f32[18,14,456]{2,1,0:T(8,128)S(1)}, u32[]{:S(2)}) copy-start(f32[18,14,456]{2,1,0:T(8,128)S(1)} %get-tuple-element.1244) | copy-start | bytes 1378948 | tf_op jit(solution)/shard_map/while
  277.2 26.3 %copy-start.1 = (f32[18,14,456]{2,1,0:T(8,128)}, f32[18,14,456]{2,1,0:T(8,128)S(1)}, u32[]{:S(2)}) copy-start(f32[18,14,456]{2,1,0:T(8,128)S(1)} %get-tuple-element.1244) | copy-start | bytes 1378948 | tf_op jit(solution)/shard_map/while
  317.0 26.3 %copy-start.1 = (f32[18,14,456]{2,1,0:T(8,128)}, f32[18,14,456]{2,1,0:T(8,128)S(1)}, u32[]{:S(2)}) copy-start(f32[18,14,456]{2,1,0:T(8,128)S(1)} %get-tuple-element.1244) | copy-start | bytes 1378948 | tf_op jit(solution)/shard_map/while
  350.7 6.1 copy-start.8
  350.7 6.1 copy-start.10
  356.8 26.3 %copy-start.1 = (f32[18,14,456]{2,1,0:T(8,128)}, f32[18,14,456]{2,1,0:T(8,128)S(1)}, u32[]{:S(2)}) copy-start(f32[18,14,456]{2,1,0:T(8,128)S(1)} %get-tuple-element.1244) | copy-start | bytes 1378948 | tf_op jit(solution)/shard_map/while
  396.5 26.3 %copy-start.1 = (f32[18,14,456]{2,1,0:T(8,128)}, f32[18,14,456]{2,1,0:T(8,128)S(1)}, u32[]{:S(2)}) copy-start(f32[18,14,456]{2,1,0:T(8,128)S(1)} %get-tuple-element.1244) | copy-start | bytes 1378948 | tf_op jit(solution)/shard_map/while
  (37 other events, 222.0 us)
where the time goes:
time: 966 us; the launch traced here: 955 us
  loops' own time  454 us (47%)
  local copies, waits for them, and re-layouts  181 us (19%)
  matrix products  168 us (17%)
  other arithmetic  125 us (13%)
  starting transfers between devices  26.1 us (3%)
    another operation x2, loops' own time, interact(): running, _ = lax.scan(advance, start, (offsets, picks))  454 us
    dot_general x20, matrix products, advance(): lax.dot_general(stacked_source, stacked_matrix, (((1,), (1,)), ((), ())),...  153 us
    concatenate x20, local copies, waits for them, and re-layouts, advance(): stacked_matrix = jnp.concatenate(matrices, axis=1)  94.5 us
    concatenate x40, other arithmetic, kernel_matrix(): return jnp.concatenate(blocks, axis=0)  64.2 us
    concatenate x20, local copies, waits for them, and re-layouts, advance(): stacked_source = jnp.concatenate(sources, axis=1)  45.9 us
    mul x30, other arithmetic, advance(): sources.append((source * weight).reshape(row_count * col_count, features))  33.2 us
    mul x20, other arithmetic, kernel_matrix(): line_blocks.append(entry * stokes_scale)  22.6 us
  transfers between devices with their start and end apart: 8, of which 0 were waited for; matrix products, arithmetic and copies ran while one was open for 20% of the time, Pallas kernels for 0%

commit v1 on v0

v1 whole, which is shorter than its diff:
```python
import functools
import itertools

import jax
import jax.numpy as jnp
import ml_dtypes
import numpy as np
from jax import lax
from jax.experimental import pallas as pl
from jax.experimental.pallas import tpu as pltpu
from jax.sharding import PartitionSpec as P

ORDER = 6
DENS = 456
TOP = 14
F32 = jnp.float32
BF16 = jnp.bfloat16
MESH = pl.DeviceIdType.MESH

ALL_OFFSETS = [(a, b) for a in range(-3, 4) for b in range(-3, 4) if max(abs(a), abs(b)) >= 2]
EVEN_OFFSETS = [(a, b) for a in range(-2, 4) for b in range(-2, 4) if max(abs(a), abs(b)) >= 2]
COUNT = len(EVEN_OFFSETS)


def rounded(values):
    return values.astype(ml_dtypes.bfloat16).astype(np.float64)


def surface_points():
    grid_line = np.linspace(-1.0, 1.0, ORDER)
    points = []
    for i in range(ORDER):
        for j in range(ORDER):
            for k in range(ORDER):
                if min(i, j, k) == 0 or max(i, j, k) == ORDER - 1:
                    points.append((grid_line[i], grid_line[j], grid_line[k]))
    return np.array(points)


def kernel_matrix(points, shift):
    r = 0.525 * (points[:, None, :] - points[None, :, :]) - np.array([shift[0], shift[1], 0.0])
    length = np.sqrt((r * r).sum(-1))
    count = len(points)
    matrix = np.zeros((3, count, 3, count))
    for a in range(3):
        for b in range(3):
            matrix[a, :, b, :] = (float(a == b) / length + r[..., a] * r[..., b] / length**3) / (8.0 * np.pi)
    return matrix.reshape(3 * count, 3 * count)


def mirror_basis(points, signs):
    count = len(points)
    place = {tuple(np.round(p * (ORDER - 1)).astype(int)): i for i, p in enumerate(points)}
    corner = [i for i, p in enumerate(points) if (p > 0).all()]
    basis = np.zeros((3 * count, 3 * len(corner)))
    for a in range(3):
        for h, i in enumerate(corner):
            for flip in itertools.product([1, -1], repeat=3):
                j = place[tuple(np.round(points[i] * np.array(flip) * (ORDER - 1)).astype(int))]
                sign = 1
                for axis in range(3):
                    if flip[axis] == -1:
                        sign *= signs[axis] * (-1 if axis == a else 1)
                basis[a * count + j, a * len(corner) + h] = sign
    return basis / np.sqrt(8.0)


@functools.lru_cache(maxsize=1)
def tables():
    points = surface_points()
    kernels = {o: kernel_matrix(points, o) for o in ALL_OFFSETS}
    stacked = np.concatenate([kernels[o] for o in ALL_OFFSETS], axis=1)
    basis = np.zeros((DENS, 512))
    sign_y = np.ones(512)
    high, low, main = [], [], []
    for t, (sx, sz) in enumerate([(1, 1), (-1, 1), (1, -1), (-1, -1)]):
        found = []
        for sy in (1, -1):
            mirror = mirror_basis(points, (sx, sy, sz))
            left, size, _ = np.linalg.svd(mirror.T @ stacked, full_matrices=False)
            for j in range(left.shape[1]):
                found.append((size[j], sy, rounded(mirror @ left[:, j])))
        found.sort(key=lambda item: -item[0])
        start = 128 * t + 32 * t
        special = range(start, start + 2 * TOP)
        rest = [lane for lane in range(128 * t, 128 * t + 128) if lane not in special]
        for j, (_, sy, column) in enumerate(found):
            lane = start + j if j < TOP else rest[j - TOP]
            basis[:, lane] = column
            sign_y[lane] = sy
            main.append(lane)
            if j < TOP:
                high.append(lane)
                low.append(lane + TOP)
                sign_y[lane + TOP] = sy
    inverse = np.linalg.inv(basis[:, main])
    doubled = basis.copy()
    doubled[:, low] = basis[:, high]
    special = np.zeros((DENS, 128))
    for t in range(4):
        special[:, 32 * t : 32 * t + 2 * TOP] = doubled[:, 160 * t : 160 * t + 2 * TOP]
    weights = np.zeros((2, COUNT, 256, 256), ml_dtypes.bfloat16)
    for k, offset in enumerate(EVEN_OFFSETS):
        core = np.zeros((512, 512))
        core[np.ix_(main, main)] = (inverse @ kernels[offset] @ inverse.T).T
        leading = core[np.ix_(high, high)]
        core[np.ix_(low, high)] = leading
        core[np.ix_(high, low)] = leading - rounded(leading)
        weights[0, k] = core[:256, :256].astype(ml_dtypes.bfloat16)
        weights[1, k] = core[256:, 256:].astype(ml_dtypes.bfloat16)
    picks = np.zeros((2, 2, len(ALL_OFFSETS), 128), ml_dtypes.bfloat16)
    for cx in range(2):
        for cy in range(2):
            for k, (a, b) in enumerate(EVEN_OFFSETS):
                offset = (-a if cx else a, -b if cy else b)
                picks[cx, cy, ALL_OFFSETS.index(offset), k] = 1
    return {
        "weights": weights.reshape(2, COUNT * 256, 256),
        "doubled": doubled.astype(ml_dtypes.bfloat16),
        "special": special.astype(ml_dtypes.bfloat16),
        "doubled_t": np.ascontiguousarray(doubled.T).astype(ml_dtypes.bfloat16),
        "special_t": np.ascontiguousarray(special.T).astype(ml_dtypes.bfloat16),
        "sign_y": np.tile(sign_y[None, :], (8, 1)).astype(np.float32),
        "picks": picks,
    }


def split(value):
    high = value.astype(BF16)
    return high, (value - high.astype(F32)).astype(BF16)


def mm(a, b):
    return jnp.dot(a, b, preferred_element_type=F32)


def mm_t(a, b):
    return lax.dot_general(a, b, (((1,), (1,)), ((), ())), preferred_element_type=F32)


def product(rows, matrix):
    rh, rl = rows
    mh, ml = matrix
    return mm_t(rh, mh) + mm_t(rl, mh) + mm_t(rh, ml)


def lanes(t):
    return slice(128 * t, 128 * t + 128)


def lane_index(shape):
    return lax.broadcasted_iota(jnp.int32, shape, len(shape) - 1)


def project(rows, doubled, special):
    high, low = split(rows)
    main = mm(high, doubled)
    fine = mm(low, special)
    place = lane_index(fine.shape)
    tiles = []
    for t in range(4):
        tile = main[:, lanes(t)]
        tile = jnp.where((place >= 32 * t) & (place < 32 * t + 32), tile + fine, tile)
        left_over = tile - tile.astype(BF16).astype(F32)
        tiles.append(jnp.where((place >= 32 * t + TOP) & (place < 32 * t + 2 * TOP), left_over, tile))
    return jnp.concatenate(tiles, axis=1)


def expand(y, doubled_t, special_t):
    high = y.astype(BF16)
    rest = y - high.astype(F32)
    place = lane_index((y.shape[0], 128))
    fine = jnp.zeros((y.shape[0], 128), F32)
    for t in range(4):
        fine = jnp.where((place >= 32 * t) & (place < 32 * t + 32), rest[:, lanes(t)], fine)
    return mm(high, doubled_t) + mm(fine.astype(BF16), special_t)


def build_shifts(padded, shifted, sign_y, width):
    blocks = padded.shape[1]
    row = lax.broadcasted_iota(jnp.int32, (blocks, width, 512), 1)
    even = lax.rem(row, 2) == 0
    signs = sign_y[0:1, :].reshape(1, 1, 512)
    for d in range(6):
        step = d - 2
        for parity in range(2):
            forward = padded[parity, :, 8 + step : 8 + step + width, :]
            backward = padded[parity, :, 8 - step : 8 - step + width, :] * signs
            shifted[d, parity] = jnp.where(even, forward, backward).astype(shifted.dtype)


def interact(shifted, lists, picks, sign_y, weights, total, half, width, group):
    count = half * width
    flags = []
    for cx in range(2):
        found = []
        for x in range(1):
            block = lists[cx].astype(F32).reshape(count, len(ALL_OFFSETS)).astype(BF16)
            found = [mm(block, picks[cx, cy]).reshape(half, width, 128) for cy in range(2)]
        row = lax.broadcasted_iota(jnp.int32, (half, width, 128), 1)
        flags.append(jnp.where(lax.rem(row, 2) == 0, found[0], found[1]))
    for first in range(0, COUNT, group):
        parts = [[], []]
        for k in range(first, min(first + group, COUNT)):
            a, b = EVEN_OFFSETS[k]
            pieces = [[] for _ in range(4)]
            for cx in range(2):
                source = cx + (-a if cx else a)
                parity, start = source % 2, source // 2 + 1
                flag = jnp.broadcast_to(flags[cx][:, :, k : k + 1], (half, width, 128)).astype(shifted.dtype)
                for t in range(4):
                    mask = -flag if (cx and t % 2) else flag
                    piece = shifted[b + 2, parity, start : start + half, :, lanes(t)] * mask
                    pieces[t].append(piece.reshape(count, 128).astype(BF16))
            for t in range(4):
                parts[t // 2].append(jnp.concatenate(pieces[t], axis=0))
        last = min(first + group, COUNT)
        for z in range(2):
            left = jnp.concatenate(parts[z], axis=1)
            term = mm(left, weights[z, first * 256 : last * 256, :])
            cols = slice(256 * z, 256 * z + 256)
            if first == 0:
                total[:, cols] = term
            else:
                total[:, cols] += term


def resigned(y, sign_y, cx, half, width):
    row = lax.broadcasted_iota(jnp.int32, (half, width, 512), 1)
    signs = sign_y[0:1, :].reshape(1, 1, 512)
    place = lane_index((1, 1, 512))
    if cx:
        turn = jnp.where(lax.rem(lax.div(place, 128), 2) == 1, -1.0, 1.0)
        return jnp.where(lax.rem(row, 2) == 0, y * turn, y * (signs * turn))
    return jnp.where(lax.rem(row, 2) == 0, y, y * signs)


DIRECTIONS = [(-1, 0), (1, 0), (0, -1), (0, 1), (-1, -1), (-1, 1), (1, -1), (1, 1)]


def pack_sides(block, strips, corners, rows, width):
    half = rows // 2
    for side in range(2):
        for col in range(2):
            y = (width - 2 if side else 0) + col
            for parity in range(2):
                for i in range(half):
                    at = parity * half + i
                    strips[side, col, at : at + 1, :] = block[2 * i + parity, y : y + 1, :]
    corners[...] = jnp.zeros_like(corners)
    for sx in range(2):
        for sy in range(2):
            for col in range(2):
                y = (width - 2 if sy else 0) + col
                for parity in range(2):
                    x = (rows - 2 if sx else 0) + parity
                    at = 2 * col + parity
                    corners[sx, sy, at : at + 1, :] = block[x, y : y + 1, :]


def side_copies(block, strips, corners, got_x, got_y, got_c, send, recv, rows, ids):
    copies = []
    for n, (dx, dy) in enumerate(DIRECTIONS):
        sx, sy = (dx + 1) // 2, (dy + 1) // 2
        if dy == 0:
            source = block.at[rows - 2 : rows] if dx > 0 else block.at[0:2]
            target = got_x.at[1 - sx]
        elif dx == 0:
            source, target = strips.at[sy], got_y.at[1 - sy]
        else:
            source, target = corners.at[sx, sy], got_c.at[1 - sx, 1 - sy]
        copies.append(
            pltpu.make_async_remote_copy(
                src_ref=source,
                dst_ref=target,
                send_sem=send.at[n],
                recv_sem=recv.at[n],
                device_id=ids[n],
                device_id_type=MESH,
            )
        )
    return copies


def fill(padded, local, got_x, got_y, got_c, held, doubled, special, rows, width, strip, chunk):
    half = rows // 2
    for c in range(0, half, chunk):
        value = local[2 * c : 2 * c + 2 * chunk].reshape(2 * chunk * width, DENS)
        value = project(value, doubled, special).reshape(chunk, 2, width, 512)
        for parity in range(2):
            padded[parity, 1 + c : 1 + c + chunk, 8 : 8 + width, :] = value[:, parity]


def fill_sides(padded, got_x, got_y, got_c, held, doubled, special, rows, width, strip):
    half = rows // 2
    value = project(got_x[...].reshape(4 * width, DENS), doubled, special).reshape(2, 2, width, 512)
    for side in range(2):
        for parity in range(2):
            padded[parity, (half + 1) * side, 8 : 8 + width, :] = value[side, parity]
    value = project(got_y[...].reshape(4 * strip, DENS), doubled, special)
    held[0 : 4 * strip, :] = value
    value = project(got_c[...].reshape(32, DENS), doubled, special)
    held[4 * strip : 4 * strip + 32, :] = value
    zero = jnp.zeros((half + 2, 8, 512), F32)
    for parity in range(2):
        padded[parity, :, 0:8, :] = zero
        padded[parity, :, 8 + width : 16 + width, :] = zero
    for side in range(2):
        for col in range(2):
            y = 8 + width + col if side else 6 + col
            for parity in range(2):
                for i in range(half):
                    at = (side * 2 + col) * strip + parity * half + i
                    padded[parity, 1 + i, y : y + 1, :] = held[at : at + 1, :]
                for sx in range(2):
                    at = 4 * strip + (sx * 2 + side) * 8 + 2 * col + parity
                    padded[parity, (half + 1) * sx, y : y + 1, :] = held[at : at + 1, :]


def body(
    sizes,
    leaf_hbm, parent_in_hbm, leaf_lists_hbm, parent_lists_hbm, up_hbm, down_hbm, inverse_hbm,
    weights_hbm, doubled_hbm, special_hbm, doubled_t_hbm, special_t_hbm, sign_hbm, picks_hbm,
    leaf_down_hbm, parent_up_hbm,
    leaf, parent_in, leaf_lists, parent_lists, up, down, inverse,
    weights, doubled, special, doubled_t, special_t, sign_y, picks,
    leaf_strips, leaf_corners, leaf_got_x, leaf_got_y, leaf_got_c, leaf_held, leaf_padded, leaf_shifted, leaf_total, leaf_check,
    parent_up, parent_strips, parent_corners, parent_got_x, parent_got_y, parent_got_c, parent_held, parent_padded,
    parent_shifted, parent_total, parent_local,
    load_sem, out_sem, leaf_send, leaf_recv, parent_send, parent_recv,
):
    rows, width, prows, pwidth, gx_size, gy_size = sizes
    half, phalf = rows // 2, prows // 2
    gx, gy = lax.axis_index("gx"), lax.axis_index("gy")
    ids = [
        (lax.rem(gx + dx + gx_size, gx_size), lax.rem(gy + dy + gy_size, gy_size)) for dx, dy in DIRECTIONS
    ]
    barrier = pltpu.get_barrier_semaphore()
    for place in ids:
        pl.semaphore_signal(barrier, inc=1, device_id=place, device_id_type=MESH)

    pairs = [(leaf_hbm, leaf)]
    pairs += [(up_hbm.at[c], up.at[c]) for c in range(4)]
    pairs += [(doubled_hbm, doubled), (special_hbm, special), (sign_hbm, sign_y), (picks_hbm, picks)]
    pairs += [(leaf_lists_hbm, leaf_lists), (weights_hbm, weights)]
    pairs += [(doubled_t_hbm, doubled_t), (special_t_hbm, special_t)]
    pairs += [(parent_lists_hbm, parent_lists), (inverse_hbm, inverse), (parent_in_hbm, parent_in), (down_hbm, down)]
    loads = [pltpu.make_async_copy(a, b, load_sem.at[n]) for n, (a, b) in enumerate(pairs)]
    for load in loads:
        load.start()

    loads[0].wait()
    pack_sides(leaf, leaf_strips, leaf_corners, rows, width)
    pl.semaphore_wait(barrier, len(DIRECTIONS))
    leaf_copies = side_copies(
        leaf, leaf_strips, leaf_corners, leaf_got_x, leaf_got_y, leaf_got_c, leaf_send, leaf_recv, rows, ids
    )
    for copy in leaf_copies:
        copy.start()

    total = jnp.zeros((phalf * 2 * pwidth, DENS), F32)
    for c in range(4):
        loads[1 + c].wait()
        child = leaf[...].reshape(prows, 2, width, DENS)[:, c // 2]
        child = child.reshape(prows, pwidth, 2, DENS)[:, :, c % 2, :].reshape(prows * pwidth, DENS)
        total = total + product(split(child), split(up[c]))
    parent_up[...] = total.reshape(prows, pwidth, DENS)
    parent_out = pltpu.make_async_copy(parent_up, parent_up_hbm, out_sem.at[0])
    parent_out.start()
    pack_sides(parent_up, parent_strips, parent_corners, prows, pwidth)
    parent_copies = side_copies(
        parent_up, parent_strips, parent_corners, parent_got_x, parent_got_y, parent_got_c,
        parent_send, parent_recv, prows, ids,
    )
    for copy in parent_copies:
        copy.start()

    for load in loads[5:10]:
        load.wait()
    fill(leaf_padded, leaf, None, None, None, None, doubled[...], special[...], rows, width, None, 3)
    for copy in leaf_copies:
        copy.wait()
    fill_sides(leaf_padded, leaf_got_x, leaf_got_y, leaf_got_c, leaf_held, doubled[...], special[...], rows, width, rows)
    build_shifts(leaf_padded, leaf_shifted, sign_y, width)
    loads[10].wait()
    loads[11].wait()
    loads[12].wait()
    lists = leaf_lists[...].reshape(half, 2, width, len(ALL_OFFSETS))
    interact(leaf_shifted, [lists[:, 0], lists[:, 1]], picks, sign_y, weights, leaf_total, half, width, 3)
    for cx in range(2):
        for c in range(0, half, 3):
            at = (cx * half + c) * width
            y = leaf_total[at : at + 3 * width, :].reshape(3, width, 512)
            y = resigned(y, sign_y, cx, 3, width).reshape(3 * width, 512)
            value = expand(y, doubled_t[...], special_t[...]).reshape(3, width, DENS)
            for i in range(3):
                leaf_check[2 * (c + i) + cx] = value[i]

    fill(parent_padded, parent_up, None, None, None, None, doubled[...], special[...], prows, pwidth, None, 6)
    for copy in parent_copies:
        copy.wait()
    fill_sides(
        parent_padded, parent_got_x, parent_got_y, parent_got_c, parent_held, doubled[...], special[...], prows, pwidth, 16
    )
    build_shifts(parent_padded, parent_shifted, sign_y, pwidth)
    for load in loads[13:]:
        load.wait()
    lists = parent_lists[...].reshape(phalf, 2, pwidth, len(ALL_OFFSETS))
    interact(parent_shifted, [lists[:, 0], lists[:, 1]], picks, sign_y, weights, parent_total, phalf, pwidth, 3)
    inverse_pair = split(inverse[...])
    for cx in range(2):
        at = cx * phalf * pwidth
        y = parent_total[at : at + phalf * pwidth, :].reshape(phalf, pwidth, 512)
        y = resigned(y, sign_y, cx, phalf, pwidth).reshape(phalf * pwidth, 512)
        value = product(split(expand(y, doubled_t[...], special_t[...])), inverse_pair).reshape(phalf, pwidth, DENS)
        for i in range(phalf):
            parent_local[2 * i + cx] = value[i] + parent_in[2 * i + cx]
    local = split(parent_local[...].reshape(prows * pwidth, DENS))
    for cx in range(2):
        sides = []
        for cy in range(2):
            sides.append(product(local, split(down[2 * cx + cy])).reshape(prows, pwidth, 1, DENS))
        both = jnp.concatenate(sides, axis=2).reshape(prows, width, DENS)
        for i in range(prows):
            leaf_check[2 * i + cx] += both[i]
    outs = []
    for c in range(4):
        at = 6 * c
        value = leaf_check[at : at + 6].reshape(6 * width, DENS)
        leaf_check[at : at + 6] = product(split(value), inverse_pair).reshape(6, width, DENS)
        out = pltpu.make_async_copy(leaf_check.at[at : at + 6], leaf_down_hbm.at[at : at + 6], out_sem.at[1 + c])
        out.start()
        outs.append(out)
    parent_out.wait()
    for out in outs:
        out.wait()


def local(sizes, leaf_up, parent_in, leaf_lists, parent_lists, up_transfer, down_transfer, check_inverse):
    rows, width, prows, pwidth = sizes[:4]
    half, phalf = rows // 2, prows // 2
    names = ("weights", "doubled", "special", "doubled_t", "special_t", "sign_y", "picks")
    constants = [jnp.asarray(tables()[name]) for name in names]
    operands = [leaf_up, parent_in, leaf_lists, parent_lists, up_transfer, down_transfer, check_inverse] + constants
    scratch = [pltpu.VMEM(x.shape, x.dtype) for x in operands]

    def sides(rows_here, width_here, strip):
        return [
            pltpu.VMEM((2, 2, strip, DENS), F32),
            pltpu.VMEM((2, 2, 8, DENS), F32),
            pltpu.VMEM((2, 2, width_here, DENS), F32),
            pltpu.VMEM((2, 2, strip, DENS), F32),
            pltpu.VMEM((2, 2, 8, DENS), F32),
            pltpu.VMEM((4 * strip + 32, 512), F32),
            pltpu.VMEM((2, rows_here // 2 + 2, 16 + width_here, 512), F32),
        ]

    scratch += sides(rows, width, rows)
    scratch += [
        pltpu.VMEM((6, 2, half + 2, width, 512), BF16),
        pltpu.VMEM((rows * width, 512), F32),
        pltpu.VMEM((rows, width, DENS), F32),
        pltpu.VMEM((prows, pwidth, DENS), F32),
    ]
    scratch += sides(prows, pwidth, 16)
    scratch += [
        pltpu.VMEM((6, 2, phalf + 2, pwidth, 512), F32),
        pltpu.VMEM((prows * pwidth, 512), F32),
        pltpu.VMEM((prows, pwidth, DENS), F32),
        pltpu.SemaphoreType.DMA((17,)),
        pltpu.SemaphoreType.DMA((5,)),
        pltpu.SemaphoreType.DMA((8,)),
        pltpu.SemaphoreType.DMA((8,)),
        pltpu.SemaphoreType.DMA((8,)),
        pltpu.SemaphoreType.DMA((8,)),
    ]
    return pl.pallas_call(
        functools.partial(body, sizes),
        out_shape=(
            jax.ShapeDtypeStruct((rows, width, DENS), F32),
            jax.ShapeDtypeStruct((prows, pwidth, DENS), F32),
        ),
        in_specs=[pl.BlockSpec(memory_space=pl.ANY)] * len(operands),
        out_specs=(pl.BlockSpec(memory_space=pl.ANY),) * 2,
        scratch_shapes=scratch,
        compiler_params=pltpu.CompilerParams(
            collective_id=0, has_side_effects=True, vmem_limit_bytes=56 * 1024 * 1024
        ),
    )(*operands)


def solution(mesh):
    gx_size, gy_size = mesh.shape["gx"], mesh.shape["gy"]
    sizes = (192 // gx_size, 256 // gy_size, 96 // gx_size, 128 // gy_size, gx_size, gy_size)
    placed = (P("gx", "gy", None),) * 4 + (P(), P(), P())
    return jax.shard_map(
        functools.partial(local, sizes),
        mesh=mesh,
        in_specs=placed,
        out_specs=(P("gx", "gy", None), P("gx", "gy", None)),
        check_vma=False,
    )
```

time: 966 us -> 32.7 us (0.03)
  the two profiles are of different devices: /device:TPU:7 before, /device:TPU:1 now
where the time goes in v1:
time: 32.7 us; the launch traced here: 32.6 us
  Pallas kernels  28.2 us (86%)
  local copies, waits for them, and re-layouts  3.7 us (11%)
  between operations  0.64 us (2%)
    pallas_call x1, Pallas kernels, local(): pl.pallas_call(functools.partial(body, sizes), out_shape=(jax.ShapeDtypeS...  28.2 us
    unnamed x2, local copies, waits for them, and re-layouts  3.7 us

profile of v1, /device:TPU:1, one launch (start us, length us, event | category | flops | bytes accessed | tf_op | source)
XLA Modules:
  0.0 32.6 jit_solution(11842788864389508644)
XLA Ops:
  0.6 28.2 %shard_map.149 = (f32[24,16,456]{2,1,0:T(8,128)}, f32[12,8,456]{2,1,0:T(8,128)}) custom-call(f32[24,16,456]{2,1,0:T(8,128)} %leaf_hbm.1, f32[12,8,456]{2,1,0:T(8,128)} %parent_in_hbm.1, s32[24,16,40]{2,1,0:T(8,128)} %leaf_lists_hbm.1, s32[12,8,40]{2,1,0:T(8,128)} %parent_lists_hbm.1, f32[4,456,456]{2,1,0:T(8,128)} %up_hbm.1, f32[4,456,456]{2,1,0:T(8,128)} %down_hbm.1, ...), custom_call_target="tpu_custom_call" | custom-call | tf_op jit(solution)/shard_map/pallas_call | solution.py:477
  28.9 2.1 %copy.18 = f32[24,16,456]{2,1,0:T(8,128)} copy(f32[24,16,456]{2,1,0:T(8,128)} %get-tuple-element.4) | data formatting | bytes 1400832
  31.0 1.6 %copy.19 = f32[12,8,456]{2,1,0:T(8,128)} copy(f32[12,8,456]{2,1,0:T(8,128)} %get-tuple-element.5) | data formatting | bytes 350208

commit v2 on v1

v2 whole, which is shorter than its diff:
```python
import functools
import itertools

import jax
import jax.numpy as jnp
import ml_dtypes
import numpy as np
from jax import lax
from jax.experimental import pallas as pl
from jax.experimental.pallas import tpu as pltpu
from jax.sharding import PartitionSpec as P

ORDER = 6
DENS = 456
TOP = 14
F32 = jnp.float32
BF16 = jnp.bfloat16
MESH = pl.DeviceIdType.MESH

ALL_OFFSETS = [(a, b) for a in range(-3, 4) for b in range(-3, 4) if max(abs(a), abs(b)) >= 2]
EVEN_OFFSETS = [(a, b) for a in range(-2, 4) for b in range(-2, 4) if max(abs(a), abs(b)) >= 2]
COUNT = len(EVEN_OFFSETS)


def rounded(values):
    return values.astype(ml_dtypes.bfloat16).astype(np.float64)


def surface_points():
    grid_line = np.linspace(-1.0, 1.0, ORDER)
    points = []
    for i in range(ORDER):
        for j in range(ORDER):
            for k in range(ORDER):
                if min(i, j, k) == 0 or max(i, j, k) == ORDER - 1:
                    points.append((grid_line[i], grid_line[j], grid_line[k]))
    return np.array(points)


def kernel_matrix(points, shift):
    r = 0.525 * (points[:, None, :] - points[None, :, :]) - np.array([shift[0], shift[1], 0.0])
    length = np.sqrt((r * r).sum(-1))
    count = len(points)
    matrix = np.zeros((3, count, 3, count))
    for a in range(3):
        for b in range(3):
            matrix[a, :, b, :] = (float(a == b) / length + r[..., a] * r[..., b] / length**3) / (8.0 * np.pi)
    return matrix.reshape(3 * count, 3 * count)


def mirror_basis(points, signs):
    count = len(points)
    place = {tuple(np.round(p * (ORDER - 1)).astype(int)): i for i, p in enumerate(points)}
    corner = [i for i, p in enumerate(points) if (p > 0).all()]
    basis = np.zeros((3 * count, 3 * len(corner)))
    for a in range(3):
        for h, i in enumerate(corner):
            for flip in itertools.product([1, -1], repeat=3):
                j = place[tuple(np.round(points[i] * np.array(flip) * (ORDER - 1)).astype(int))]
                sign = 1
                for axis in range(3):
                    if flip[axis] == -1:
                        sign *= signs[axis] * (-1 if axis == a else 1)
                basis[a * count + j, a * len(corner) + h] = sign
    return basis / np.sqrt(8.0)


@functools.lru_cache(maxsize=1)
def tables():
    points = surface_points()
    kernels = {o: kernel_matrix(points, o) for o in ALL_OFFSETS}
    stacked = np.concatenate([kernels[o] for o in ALL_OFFSETS], axis=1)
    basis = np.zeros((DENS, 512))
    sign_y = np.ones(512)
    high, low, main = [], [], []
    for t, (sx, sz) in enumerate([(1, 1), (-1, 1), (1, -1), (-1, -1)]):
        found = []
        for sy in (1, -1):
            mirror = mirror_basis(points, (sx, sy, sz))
            left, size, _ = np.linalg.svd(mirror.T @ stacked, full_matrices=False)
            for j in range(left.shape[1]):
                found.append((size[j], sy, rounded(mirror @ left[:, j])))
        found.sort(key=lambda item: -item[0])
        start = 128 * t + 32 * t
        special = range(start, start + 2 * TOP)
        rest = [lane for lane in range(128 * t, 128 * t + 128) if lane not in special]
        for j, (_, sy, column) in enumerate(found):
            lane = start + j if j < TOP else rest[j - TOP]
            basis[:, lane] = column
            sign_y[lane] = sy
            main.append(lane)
            if j < TOP:
                high.append(lane)
                low.append(lane + TOP)
                sign_y[lane + TOP] = sy
    inverse = np.linalg.inv(basis[:, main])
    doubled = basis.copy()
    doubled[:, low] = basis[:, high]
    special = np.zeros((DENS, 128))
    for t in range(4):
        special[:, 32 * t : 32 * t + 2 * TOP] = doubled[:, 160 * t : 160 * t + 2 * TOP]
    weights = np.zeros((2, COUNT, 256, 256), ml_dtypes.bfloat16)
    for k, offset in enumerate(EVEN_OFFSETS):
        core = np.zeros((512, 512))
        core[np.ix_(main, main)] = (inverse @ kernels[offset] @ inverse.T).T
        leading = core[np.ix_(high, high)]
        core[np.ix_(low, high)] = leading
        core[np.ix_(high, low)] = leading - rounded(leading)
        weights[0, k] = core[:256, :256].astype(ml_dtypes.bfloat16)
        weights[1, k] = core[256:, 256:].astype(ml_dtypes.bfloat16)
    picks = np.zeros((2, 2, len(ALL_OFFSETS), 128), ml_dtypes.bfloat16)
    for cx in range(2):
        for cy in range(2):
            for k, (a, b) in enumerate(EVEN_OFFSETS):
                offset = (-a if cx else a, -b if cy else b)
                picks[cx, cy, ALL_OFFSETS.index(offset), k] = 1
    return {
        "weights": weights.reshape(2, COUNT * 256, 256),
        "doubled": doubled.astype(ml_dtypes.bfloat16),
        "special": special.astype(ml_dtypes.bfloat16),
        "doubled_t": np.ascontiguousarray(doubled.T).astype(ml_dtypes.bfloat16),
        "special_t": np.ascontiguousarray(special.T).astype(ml_dtypes.bfloat16),
        "sign_y": np.tile(sign_y[None, :], (8, 1)).astype(np.float32),
        "picks": picks,
    }


def split(value):
    high = value.astype(BF16)
    return high, (value - high.astype(F32)).astype(BF16)


def mm(a, b):
    return jnp.dot(a, b, preferred_element_type=F32)


def mm_t(a, b):
    return lax.dot_general(a, b, (((1,), (1,)), ((), ())), preferred_element_type=F32)


def product(rows, high_matrix, low_matrix):
    count = rows.shape[0]
    high, low = split(rows)
    both = mm_t(jnp.concatenate([high, low], axis=0), high_matrix)
    return both[:count] + both[count:] + mm_t(high, low_matrix)


def lanes(t):
    return slice(128 * t, 128 * t + 128)


def lane_index(shape):
    return lax.broadcasted_iota(jnp.int32, shape, len(shape) - 1)


def project(rows, doubled, special):
    high, low = split(rows)
    main = mm(high, doubled)
    fine = mm(low, special)
    place = lane_index(fine.shape)
    tiles = []
    for t in range(4):
        tile = main[:, lanes(t)]
        tile = jnp.where((place >= 32 * t) & (place < 32 * t + 32), tile + fine, tile)
        left_over = tile - tile.astype(BF16).astype(F32)
        tiles.append(jnp.where((place >= 32 * t + TOP) & (place < 32 * t + 2 * TOP), left_over, tile))
    return jnp.concatenate(tiles, axis=1)


def expand(y, doubled_t, special_t):
    high = y.astype(BF16)
    rest = y - high.astype(F32)
    place = lane_index((y.shape[0], 128))
    fine = jnp.zeros((y.shape[0], 128), F32)
    for t in range(4):
        fine = jnp.where((place >= 32 * t) & (place < 32 * t + 32), rest[:, lanes(t)], fine)
    return mm(high, doubled_t) + mm(fine.astype(BF16), special_t)


def turned(shape):
    return jnp.where(lax.rem(lax.div(lane_index(shape), 128), 2) == 1, -1.0, 1.0)


DIRECTIONS = [(-1, 0), (1, 0), (0, -1), (0, 1), (-1, -1), (-1, 1), (1, -1), (1, 1)]


def pack_sides(row_of, strips, corners, rows, width):
    half = rows // 2
    for side in range(2):
        for col in range(2):
            y = (width - 2 if side else 0) + col
            for parity in range(2):
                for i in range(half):
                    at = parity * half + i
                    strips[side, col, at : at + 1, :] = row_of(2 * i + parity, y)
    corners[...] = jnp.zeros_like(corners)
    for sx in range(2):
        for sy in range(2):
            for col in range(2):
                y = (width - 2 if sy else 0) + col
                for parity in range(2):
                    x = (rows - 2 if sx else 0) + parity
                    at = 2 * col + parity
                    corners[sx, sy, at : at + 1, :] = row_of(x, y)


def side_copies(block, strips, corners, got_x, got_y, got_c, send, recv, rows, ids):
    copies = []
    for n, (dx, dy) in enumerate(DIRECTIONS):
        sx, sy = (dx + 1) // 2, (dy + 1) // 2
        if dy == 0:
            source = block.at[rows - 2 : rows] if dx > 0 else block.at[0:2]
            target = got_x.at[1 - sx]
        elif dx == 0:
            source, target = strips.at[sy], got_y.at[1 - sy]
        else:
            source, target = corners.at[sx, sy], got_c.at[1 - sx, 1 - sy]
        copies.append(
            pltpu.make_async_remote_copy(
                src_ref=source,
                dst_ref=target,
                send_sem=send.at[n],
                recv_sem=recv.at[n],
                device_id=ids[n],
                device_id_type=MESH,
            )
        )
    return copies


def hold_sides(held, got_y, got_c, doubled, special, strip):
    held[0 : 4 * strip, :] = project(got_y[...].reshape(4 * strip, DENS), doubled, special)
    held[4 * strip : 4 * strip + 32, :] = project(got_c[...].reshape(32, DENS), doubled, special)


def place_sides(put, held, half, strip):
    for side in range(2):
        for col in range(2):
            for parity in range(2):
                for i in range(half):
                    at = (side * 2 + col) * strip + parity * half + i
                    put(parity, 1 + i, side, col, held[at : at + 1, :])
                for sx in range(2):
                    at = 4 * strip + (sx * 2 + side) * 8 + 2 * col + parity
                    put(parity, (half + 1) * sx, side, col, held[at : at + 1, :])


def fill_leaf(padded, children, doubled, special, rows, chunk):
    half = rows // 2
    places = children.shape[2]
    for c in range(0, half, chunk):
        value = children[2 * c : 2 * c + 2 * chunk].reshape(4 * chunk * places, DENS)
        value = project(value, doubled, special).reshape(chunk, 2, 2, places, 512)
        for parity in range(2):
            padded[parity, 1 + c : 1 + c + chunk, :, 8 : 8 + places, :] = value[:, parity]


def fill_leaf_sides(padded, got_x, got_y, got_c, held, doubled, special, rows, places, strip):
    half = rows // 2
    value = project(got_x[...].reshape(8 * places, DENS), doubled, special).reshape(2, 2, 2, places, 512)
    for side in range(2):
        for parity in range(2):
            padded[parity, (half + 1) * side, :, 8 : 8 + places, :] = value[side, parity]
    hold_sides(held, got_y, got_c, doubled, special, strip)

    def put(parity, x, side, col, row):
        y = 8 + places if side else 7
        padded[parity, x, col, y : y + 1, :] = row

    place_sides(put, held, half, strip)


def shift_leaf(padded, shifted, sign_y, places):
    signs = sign_y[0:1, :].reshape(1, 1, 512)
    for d in range(6):
        step = d - 2
        for parity in range(2):
            found = []
            for target in range(2):
                source = target + (-step if target else step)
                start = 8 + source // 2
                value = padded[parity, :, source % 2, start : start + places, :]
                found.append(value * signs if target else value)
            shifted[d, parity] = jnp.concatenate(found, axis=1).astype(BF16)


def fill_parent(padded, block, doubled, special, rows, width):
    half = rows // 2
    value = project(block[...].reshape(rows * width, DENS), doubled, special).reshape(half, 2, width, 512)
    for parity in range(2):
        padded[parity, 1 : 1 + half, 8 : 8 + width, :] = value[:, parity]
    zero = jnp.zeros((half + 2, 8, 512), F32)
    for parity in range(2):
        padded[parity, :, 0:8, :] = zero
        padded[parity, :, 8 + width : 16 + width, :] = zero


def fill_parent_sides(padded, got_x, got_y, got_c, held, doubled, special, rows, width, strip):
    half = rows // 2
    value = project(got_x[...].reshape(4 * width, DENS), doubled, special).reshape(2, 2, width, 512)
    for side in range(2):
        for parity in range(2):
            padded[parity, (half + 1) * side, 8 : 8 + width, :] = value[side, parity]
    hold_sides(held, got_y, got_c, doubled, special, strip)

    def put(parity, x, side, col, row):
        y = 8 + width + col if side else 6 + col
        padded[parity, x, y : y + 1, :] = row

    place_sides(put, held, half, strip)


def shift_parent(padded, shifted, sign_y, width):
    row = lax.broadcasted_iota(jnp.int32, (padded.shape[1], width, 512), 1)
    even = lax.rem(row, 2) == 0
    signs = sign_y[0:1, :].reshape(1, 1, 512)
    for d in range(6):
        step = d - 2
        for parity in range(2):
            forward = padded[parity, :, 8 + step : 8 + step + width, :]
            backward = padded[parity, :, 8 - step : 8 - step + width, :] * signs
            shifted[d, parity] = jnp.where(even, forward, backward)


def leaf_flags(lists, picks, rows, width):
    half, places = rows // 2, width // 2
    block = lists[...].astype(F32).reshape(half, 2, places, 2, len(ALL_OFFSETS))
    found = []
    for cx in range(2):
        pair = []
        for cy in range(2):
            part = block[:, cx, :, cy, :].reshape(half * places, len(ALL_OFFSETS)).astype(BF16)
            pair.append(mm(part, picks[cx, cy]).reshape(half, places, 128))
        found.append(jnp.concatenate(pair, axis=1))
    return found


def parent_flags(lists, picks, rows, width):
    half = rows // 2
    block = lists[...].astype(F32).reshape(half, 2, width, len(ALL_OFFSETS))
    even = lax.rem(lax.broadcasted_iota(jnp.int32, (half, width, 128), 1), 2) == 0
    found = []
    for cx in range(2):
        part = block[:, cx].reshape(half * width, len(ALL_OFFSETS)).astype(BF16)
        pair = [mm(part, picks[cx, cy]).reshape(half, width, 128) for cy in range(2)]
        found.append(jnp.where(even, pair[0], pair[1]))
    return found


def interact(levels, weights, total, group):
    for first in range(0, COUNT, group):
        last = min(first + group, COUNT)
        parts = [[], []]
        for k in range(first, last):
            a, b = EVEN_OFFSETS[k]
            pieces = [[] for _ in range(4)]
            for shifted, flags, half, width in levels:
                for cx in range(2):
                    source = cx + (-a if cx else a)
                    parity, start = source % 2, source // 2 + 1
                    flag = flags[cx, :, :, k : k + 1]
                    flag = jnp.broadcast_to(flag, (half, width, 128)).astype(shifted.dtype)
                    for t in range(4):
                        mask = -flag if (cx and t % 2) else flag
                        piece = shifted[b + 2, parity, start : start + half, :, lanes(t)] * mask
                        pieces[t].append(piece.reshape(half * width, 128).astype(BF16))
            for t in range(4):
                parts[t // 2].append(jnp.concatenate(pieces[t], axis=0))
        for z in range(2):
            term = mm(jnp.concatenate(parts[z], axis=1), weights[z, first * 256 : last * 256, :])
            cols = slice(256 * z, 256 * z + 256)
            if first == 0:
                total[:, cols] = term
            else:
                total[:, cols] += term


def near_body(
    sizes,
    leaf_hbm, parent_in_hbm, leaf_lists_hbm, parent_lists_hbm, up_hbm, down_hbm, inverse_hbm,
    weights_hbm, doubled_hbm, special_hbm, doubled_t_hbm, special_t_hbm, sign_hbm, picks_hbm,
    leaf_check, parent_up,
    leaf, parent_in, leaf_lists, parent_lists, up, down, inverse,
    weights, doubled, special, doubled_t, special_t, sign_y, picks,
    down_high, down_low, inverse_high, inverse_low,
    leaf_strips, leaf_corners, leaf_got_x, leaf_got_y, leaf_got_c, leaf_held,
    parent_strips, parent_corners, parent_got_x, parent_got_y, parent_got_c, parent_held,
    children, leaf_padded, leaf_shifted, leaf_marks,
    parent_padded, parent_shifted, parent_marks, parent_local, total,
    load_sem, leaf_send, leaf_recv, parent_send, parent_recv,
):
    rows, width, prows, pwidth, gx_size, gy_size = sizes
    half, phalf = rows // 2, prows // 2
    places = width // 2
    gx, gy = lax.axis_index("gx"), lax.axis_index("gy")
    ids = [
        (lax.rem(gx + dx + gx_size, gx_size), lax.rem(gy + dy + gy_size, gy_size)) for dx, dy in DIRECTIONS
    ]
    barrier = pltpu.get_barrier_semaphore()
    for place in ids:
        pl.semaphore_signal(barrier, inc=1, device_id=place, device_id_type=MESH)

    pairs = [(leaf_hbm, leaf)]
    pairs += [(up_hbm.at[c], up.at[c]) for c in range(4)]
    pairs += [(doubled_hbm, doubled), (special_hbm, special), (sign_hbm, sign_y), (picks_hbm, picks)]
    pairs += [(leaf_lists_hbm, leaf_lists), (parent_lists_hbm, parent_lists)]
    pairs += [(down_hbm, down), (inverse_hbm, inverse), (weights_hbm, weights)]
    pairs += [(doubled_t_hbm, doubled_t), (special_t_hbm, special_t), (parent_in_hbm, parent_in)]
    loads = [pltpu.make_async_copy(a, b, load_sem.at[n]) for n, (a, b) in enumerate(pairs)]
    for load in loads:
        load.start()

    loads[0].wait()
    for cy in range(2):
        children[:, cy] = leaf[...].reshape(rows, places, 2, DENS)[:, :, cy, :]
    pack_sides(lambda x, y: leaf[x, y : y + 1, :], leaf_strips, leaf_corners, rows, width)
    for c in range(4):
        loads[1 + c].wait()
        child = children[...].reshape(prows, 2, 2, pwidth, DENS)[:, c // 2, c % 2].reshape(prows * pwidth, DENS)
        term = product(child, *split(up[c])).reshape(prows, pwidth, DENS)
        if c == 0:
            parent_up[...] = term
        else:
            parent_up[...] += term
    pack_sides(lambda x, y: parent_up[x, y : y + 1, :], parent_strips, parent_corners, prows, pwidth)
    pl.semaphore_wait(barrier, len(DIRECTIONS))
    leaf_copies = side_copies(
        children, leaf_strips, leaf_corners, leaf_got_x, leaf_got_y, leaf_got_c, leaf_send, leaf_recv, rows, ids
    )
    parent_copies = side_copies(
        parent_up, parent_strips, parent_corners, parent_got_x, parent_got_y, parent_got_c,
        parent_send, parent_recv, prows, ids,
    )
    for copy in leaf_copies + parent_copies:
        copy.start()

    for load in loads[5:13]:
        load.wait()
    basis = (doubled[...], special[...])
    fill_leaf(leaf_padded, children, *basis, rows, 3)
    fill_parent(parent_padded, parent_up, *basis, prows, pwidth)
    for cx, value in enumerate(leaf_flags(leaf_lists, picks, rows, width)):
        leaf_marks[cx] = value
    for cx, value in enumerate(parent_flags(parent_lists, picks, prows, pwidth)):
        parent_marks[cx] = value
    for c in range(4):
        down_high[c], down_low[c] = split(down[c])
    inverse_high[...], inverse_low[...] = split(inverse[...])
    for load in loads[13:]:
        load.wait()
    for copy in leaf_copies:
        copy.wait()
    fill_leaf_sides(leaf_padded, leaf_got_x, leaf_got_y, leaf_got_c, leaf_held, *basis, rows, places, rows)
    shift_leaf(leaf_padded, leaf_shifted, sign_y, places)
    for copy in parent_copies:
        copy.wait()
    fill_parent_sides(
        parent_padded, parent_got_x, parent_got_y, parent_got_c, parent_held, *basis, prows, pwidth, 16
    )
    shift_parent(parent_padded, parent_shifted, sign_y, pwidth)
    levels = [(leaf_shifted, leaf_marks, half, width), (parent_shifted, parent_marks, phalf, pwidth)]
    interact(levels, weights, total, 3)

    signs = sign_y[0:1, :].reshape(1, 1, 512)
    leaf_count, parent_count = rows * width, prows * pwidth
    y = total[leaf_count : leaf_count + parent_count, :].reshape(2, phalf, pwidth, 512)
    row = lax.broadcasted_iota(jnp.int32, (phalf, pwidth, 512), 1)
    y = [jnp.where(lax.rem(row, 2) == 0, part, part * signs) for part in (y[0], y[1] * turned((1, 1, 512)))]
    y = jnp.concatenate(y, axis=0).reshape(parent_count, 512)
    value = product(expand(y, doubled_t[...], special_t[...]), inverse_high[...], inverse_low[...])
    value = value.reshape(2, phalf, pwidth, DENS)
    for cx in range(2):
        for i in range(phalf):
            parent_local[2 * i + cx] = value[cx, i] + parent_in[2 * i + cx]

    quarter = leaf_count // 4
    for c in range(4):
        y = total[c * quarter : (c + 1) * quarter, :].reshape(half // 2, 2, places, 512)
        if c >= 2:
            y = y * turned((1, 1, 1, 512))
        y = jnp.concatenate([y[:, 0:1], y[:, 1:2] * signs.reshape(1, 1, 1, 512)], axis=1).reshape(quarter, 512)
        value = expand(y, doubled_t[...], special_t[...]).reshape(half // 2, 2, places, DENS)
        for i in range(half // 2):
            leaf_check[2 * (i + (c % 2) * (half // 2)) + c // 2] = value[i]

    local = parent_local[...].reshape(parent_count, DENS)
    for c in range(4):
        value = product(local, down_high[c], down_low[c]).reshape(prows, pwidth, DENS)
        for i in range(prows):
            leaf_check[2 * i + c // 2, c % 2] += value[i]


def last_body(check, parent_up, inverse, leaf_down, parent_out):
    rows, _, places, _ = check.shape
    parent_out[...] = parent_up[...]
    value = product(check[...].reshape(rows * 2 * places, DENS), *split(inverse[...]))
    value = value.reshape(rows, 2, places, DENS)
    pair = [value[:, cy].reshape(rows, places, 1, DENS) for cy in range(2)]
    leaf_down[...] = jnp.concatenate(pair, axis=2).reshape(rows, 2 * places, DENS)


def local(sizes, leaf_up, parent_in, leaf_lists, parent_lists, up_transfer, down_transfer, check_inverse):
    rows, width, prows, pwidth = sizes[:4]
    half, phalf = rows // 2, prows // 2
    places = width // 2
    names = ("weights", "doubled", "special", "doubled_t", "special_t", "sign_y", "picks")
    constants = [jnp.asarray(tables()[name]) for name in names]
    operands = [leaf_up, parent_in, leaf_lists, parent_lists, up_transfer, down_transfer, check_inverse] + constants
    scratch = [pltpu.VMEM(x.shape, x.dtype) for x in operands]
    scratch += [pltpu.VMEM((4, DENS, DENS), BF16)] * 2 + [pltpu.VMEM((DENS, DENS), BF16)] * 2

    def sides(x_shape, strip):
        return [
            pltpu.VMEM((2, 2, strip, DENS), F32),
            pltpu.VMEM((2, 2, 8, DENS), F32),
            pltpu.VMEM((2, 2) + x_shape + (DENS,), F32),
            pltpu.VMEM((2, 2, strip, DENS), F32),
            pltpu.VMEM((2, 2, 8, DENS), F32),
            pltpu.VMEM((4 * strip + 32, 512), F32),
        ]

    scratch += sides((2, places), rows) + sides((pwidth,), 16)
    scratch += [
        pltpu.VMEM((rows, 2, places, DENS), F32),
        pltpu.VMEM((2, half + 2, 2, 16 + places, 512), F32),
        pltpu.VMEM((6, 2, half + 2, width, 512), BF16),
        pltpu.VMEM((2, half, width, 128), F32),
        pltpu.VMEM((2, phalf + 2, 16 + pwidth, 512), F32),
        pltpu.VMEM((6, 2, phalf + 2, pwidth, 512), F32),
        pltpu.VMEM((2, phalf, pwidth, 128), F32),
        pltpu.VMEM((prows, pwidth, DENS), F32),
        pltpu.VMEM((rows * width + prows * pwidth, 512), F32),
        pltpu.SemaphoreType.DMA((17,)),
        pltpu.SemaphoreType.DMA((8,)),
        pltpu.SemaphoreType.DMA((8,)),
        pltpu.SemaphoreType.DMA((8,)),
        pltpu.SemaphoreType.DMA((8,)),
    ]
    check, parent_up = pl.pallas_call(
        functools.partial(near_body, sizes),
        out_shape=(
            pltpu.VMEM((rows, 2, places, DENS), F32),
            pltpu.VMEM((prows, pwidth, DENS), F32),
        ),
        in_specs=[pl.BlockSpec(memory_space=pltpu.HBM)] * len(operands),
        out_specs=(pl.BlockSpec(memory_space=pltpu.VMEM),) * 2,
        scratch_shapes=scratch,
        compiler_params=pltpu.CompilerParams(
            collective_id=0, has_side_effects=True, vmem_limit_bytes=60 * 1024 * 1024
        ),
    )(*operands)
    return pl.pallas_call(
        last_body,
        out_shape=(
            jax.ShapeDtypeStruct((rows, width, DENS), F32),
            jax.ShapeDtypeStruct((prows, pwidth, DENS), F32),
        ),
        in_specs=[pl.BlockSpec(memory_space=pltpu.VMEM)] * 3,
        out_specs=(pl.BlockSpec(memory_space=pltpu.VMEM),) * 2,
        compiler_params=pltpu.CompilerParams(vmem_limit_bytes=16 * 1024 * 1024),
    )(check, parent_up, check_inverse)


def solution(mesh):
    gx_size, gy_size = mesh.shape["gx"], mesh.shape["gy"]
    sizes = (192 // gx_size, 256 // gy_size, 96 // gx_size, 128 // gy_size, gx_size, gy_size)
    placed = (P("gx", "gy", None),) * 4 + (P(), P(), P())
    return jax.shard_map(
        functools.partial(local, sizes),
        mesh=mesh,
        in_specs=placed,
        out_specs=(P("gx", "gy", None), P("gx", "gy", None)),
        check_vma=False,
    )
```

time: 32.7 us -> 26.8 us (0.82)
  the two profiles are of different devices: /device:TPU:1 before, /device:TPU:0 now
where the time goes in v2:
time: 26.8 us; the launch traced here: 26.7 us
  Pallas kernels  26 us (97%)
  between operations  0.66 us (2%)
    pallas_call x1, Pallas kernels, local(): pl.pallas_call(functools.partial(near_body, sizes), out_shape=(pltpu.VMEM...  23.8 us
    pallas_call x1, Pallas kernels, local(): pl.pallas_call(last_body, out_shape=(jax.ShapeDtypeStruct((rows, width, D...  2.24 us

profile of v2, /device:TPU:0, one launch (start us, length us, event | category | flops | bytes accessed | tf_op | source)
XLA Modules:
  0.0 26.7 jit_solution(4044947304142324786)
XLA Ops:
  0.6 0.0 copy-start
  0.6 23.8 %shard_map.149 = (f32[24,2,8,456]{3,2,1,0:T(8,128)S(1)}, f32[12,8,456]{2,1,0:T(8,128)S(1)}) custom-call(f32[24,16,456]{2,1,0:T(8,128)} %leaf_hbm.1, f32[12,8,456]{2,1,0:T(8,128)} %parent_in_hbm.1, s32[24,16,40]{2,1,0:T(8,128)} %leaf_lists_hbm.1, s32[12,8,40]{2,1,0:T(8,128)} %parent_lists_hbm.1, f32[4,456,456]{2,1,0:T(8,128)} %up_hbm.1, ...), custom_call_target="tpu_custom_call" | custom-call | tf_op jit(solution)/shard_map/pallas_call | solution.py:539
  24.5 0.0 copy-done
  24.5 2.2 %shard_map.150 = (f32[24,16,456]{2,1,0:T(8,128)}, f32[12,8,456]{2,1,0:T(8,128)}) custom-call(f32[24,2,8,456]{3,2,1,0:T(8,128)S(1)} %get-tuple-element.4.check, f32[12,8,456]{2,1,0:T(8,128)S(1)} %get-tuple-element.5.parent_up, f32[456,456]{1,0:T(8,128)S(1)} %copy-done), custom_call_target="tpu_custom_call" | custom-call | tf_op jit(solution)/shard_map/pallas_call | solution.py:552
Async XLA Ops:
  0.6 23.8 %copy-start = (f32[456,456]{1,0:T(8,128)S(1)}, f32[456,456]{1,0:T(8,128)}, u32[]{:S(2)}) copy-start(f32[456,456]{1,0:T(8,128)} %inverse.1) | copy-start | bytes 2495236

commit v3 on v2

--- a/solution.py
+++ b/solution.py
@@ -191,9 +191,8 @@
             y = (width - 2 if side else 0) + col
             for parity in range(2):
                 for i in range(half):
-                    at = parity * half + i
-                    strips[side, col, at : at + 1, :] = row_of(2 * i + parity, y)
-    corners[...] = jnp.zeros_like(corners)
+                    at = col * rows + parity * half + i
+                    strips[side, at : at + 1, :] = row_of(2 * i + parity, y)
     for sx in range(2):
         for sy in range(2):
             for col in range(2):
@@ -228,20 +227,22 @@
     return copies
 
 
-def hold_sides(held, got_y, got_c, doubled, special, strip):
-    held[0 : 4 * strip, :] = project(got_y[...].reshape(4 * strip, DENS), doubled, special)
-    held[4 * strip : 4 * strip + 32, :] = project(got_c[...].reshape(32, DENS), doubled, special)
-
-
-def place_sides(put, held, half, strip):
+def project_sides(held, got_x, got_y, got_c, doubled, special):
+    parts = [got_x[...].reshape(-1, DENS), got_y[...].reshape(-1, DENS)]
+    parts += [got_c[sx, sy] for sx in range(2) for sy in range(2)]
+    held[...] = project(jnp.concatenate(parts, axis=0), doubled, special)
+
+
+def place_sides(put, held, first, rows):
+    half = rows // 2
     for side in range(2):
         for col in range(2):
             for parity in range(2):
                 for i in range(half):
-                    at = (side * 2 + col) * strip + parity * half + i
+                    at = first + (side * 2 + col) * rows + parity * half + i
                     put(parity, 1 + i, side, col, held[at : at + 1, :])
                 for sx in range(2):
-                    at = 4 * strip + (sx * 2 + side) * 8 + 2 * col + parity
+                    at = first + 4 * rows + (sx * 2 + side) * 4 + 2 * col + parity
                     put(parity, (half + 1) * sx, side, col, held[at : at + 1, :])
 
 
@@ -255,19 +256,18 @@
             padded[parity, 1 + c : 1 + c + chunk, :, 8 : 8 + places, :] = value[:, parity]
 
 
-def fill_leaf_sides(padded, got_x, got_y, got_c, held, doubled, special, rows, places, strip):
-    half = rows // 2
-    value = project(got_x[...].reshape(8 * places, DENS), doubled, special).reshape(2, 2, 2, places, 512)
+def fill_leaf_sides(padded, held, rows, places):
+    half = rows // 2
+    value = held[0 : 8 * places, :].reshape(2, 2, 2, places, 512)
     for side in range(2):
         for parity in range(2):
             padded[parity, (half + 1) * side, :, 8 : 8 + places, :] = value[side, parity]
-    hold_sides(held, got_y, got_c, doubled, special, strip)
 
     def put(parity, x, side, col, row):
         y = 8 + places if side else 7
         padded[parity, x, col, y : y + 1, :] = row
 
-    place_sides(put, held, half, strip)
+    place_sides(put, held, 8 * places, rows)
 
 
 def shift_leaf(padded, shifted, sign_y, places):
@@ -295,19 +295,18 @@
         padded[parity, :, 8 + width : 16 + width, :] = zero
 
 
-def fill_parent_sides(padded, got_x, got_y, got_c, held, doubled, special, rows, width, strip):
-    half = rows // 2
-    value = project(got_x[...].reshape(4 * width, DENS), doubled, special).reshape(2, 2, width, 512)
+def fill_parent_sides(padded, held, rows, width):
+    half = rows // 2
+    value = held[0 : 4 * width, :].reshape(2, 2, width, 512)
     for side in range(2):
         for parity in range(2):
             padded[parity, (half + 1) * side, 8 : 8 + width, :] = value[side, parity]
-    hold_sides(held, got_y, got_c, doubled, special, strip)
 
     def put(parity, x, side, col, row):
         y = 8 + width + col if side else 6 + col
         padded[parity, x, y : y + 1, :] = row
 
-    place_sides(put, held, half, strip)
+    place_sides(put, held, 4 * width, rows)
 
 
 def shift_parent(padded, shifted, sign_y, width):
@@ -379,10 +378,10 @@
     sizes,
     leaf_hbm, parent_in_hbm, leaf_lists_hbm, parent_lists_hbm, up_hbm, down_hbm, inverse_hbm,
     weights_hbm, doubled_hbm, special_hbm, doubled_t_hbm, special_t_hbm, sign_hbm, picks_hbm,
-    leaf_check, parent_up,
+    leaf_check, parent_up, inverse_high, inverse_low,
     leaf, parent_in, leaf_lists, parent_lists, up, down, inverse,
     weights, doubled, special, doubled_t, special_t, sign_y, picks,
-    down_high, down_low, inverse_high, inverse_low,
+    down_high, down_low,
     leaf_strips, leaf_corners, leaf_got_x, leaf_got_y, leaf_got_c, leaf_held,
     parent_strips, parent_corners, parent_got_x, parent_got_y, parent_got_c, parent_held,
     children, leaf_padded, leaf_shifted, leaf_marks,
@@ -414,6 +413,12 @@
     for cy in range(2):
         children[:, cy] = leaf[...].reshape(rows, places, 2, DENS)[:, :, cy, :]
     pack_sides(lambda x, y: leaf[x, y : y + 1, :], leaf_strips, leaf_corners, rows, width)
+    pl.semaphore_wait(barrier, len(DIRECTIONS))
+    leaf_copies = side_copies(
+        children, leaf_strips, leaf_corners, leaf_got_x, leaf_got_y, leaf_got_c, leaf_send, leaf_recv, rows, ids
+    )
+    for copy in leaf_copies:
+        copy.start()
     for c in range(4):
         loads[1 + c].wait()
         child = children[...].reshape(prows, 2, 2, pwidth, DENS)[:, c // 2, c % 2].reshape(prows * pwidth, DENS)
@@ -423,15 +428,11 @@
         else:
             parent_up[...] += term
     pack_sides(lambda x, y: parent_up[x, y : y + 1, :], parent_strips, parent_corners, prows, pwidth)
-    pl.semaphore_wait(barrier, len(DIRECTIONS))
-    leaf_copies = side_copies(
-        children, leaf_strips, leaf_corners, leaf_got_x, leaf_got_y, leaf_got_c, leaf_send, leaf_recv, rows, ids
-    )
     parent_copies = side_copies(
         parent_up, parent_strips, parent_corners, parent_got_x, parent_got_y, parent_got_c,
         parent_send, parent_recv, prows, ids,
     )
-    for copy in leaf_copies + parent_copies:
+    for copy in parent_copies:
         copy.start()
 
     for load in loads[5:13]:
@@ -450,13 +451,13 @@
         load.wait()
     for copy in leaf_copies:
         copy.wait()
-    fill_leaf_sides(leaf_padded, leaf_got_x, leaf_got_y, leaf_got_c, leaf_held, *basis, rows, places, rows)
+    project_sides(leaf_held, leaf_got_x, leaf_got_y, leaf_got_c, *basis)
+    fill_leaf_sides(leaf_padded, leaf_held, rows, places)
     shift_leaf(leaf_padded, leaf_shifted, sign_y, places)
     for copy in parent_copies:
         copy.wait()
-    fill_parent_sides(
-        parent_padded, parent_got_x, parent_got_y, parent_got_c, parent_held, *basis, prows, pwidth, 16
-    )
+    project_sides(parent_held, parent_got_x, parent_got_y, parent_got_c, *basis)
+    fill_parent_sides(parent_padded, parent_held, prows, pwidth)
     shift_parent(parent_padded, parent_shifted, sign_y, pwidth)
     levels = [(leaf_shifted, leaf_marks, half, width), (parent_shifted, parent_marks, phalf, pwidth)]
     interact(levels, weights, total, 3)
@@ -490,13 +491,21 @@
             leaf_check[2 * i + c // 2, c % 2] += value[i]
 
 
-def last_body(check, parent_up, inverse, leaf_down, parent_out):
+def last_body(check, parent_up, high, low, leaf_down_hbm, parent_up_hbm, leaf_down, sem):
     rows, _, places, _ = check.shape
-    parent_out[...] = parent_up[...]
-    value = product(check[...].reshape(rows * 2 * places, DENS), *split(inverse[...]))
-    value = value.reshape(rows, 2, places, DENS)
-    pair = [value[:, cy].reshape(rows, places, 1, DENS) for cy in range(2)]
-    leaf_down[...] = jnp.concatenate(pair, axis=2).reshape(rows, 2 * places, DENS)
+    copies = [pltpu.make_async_copy(parent_up, parent_up_hbm, sem.at[0])]
+    copies[0].start()
+    part = rows // 2
+    for c in range(2):
+        here = slice(part * c, part * c + part)
+        value = product(check[here].reshape(part * 2 * places, DENS), high[...], low[...])
+        value = value.reshape(part, 2, places, DENS)
+        pair = [value[:, cy].reshape(part, places, 1, DENS) for cy in range(2)]
+        leaf_down[here] = jnp.concatenate(pair, axis=2).reshape(part, 2 * places, DENS)
+        copies.append(pltpu.make_async_copy(leaf_down.at[here], leaf_down_hbm.at[here], sem.at[1 + c]))
+        copies[-1].start()
+    for copy in copies:
+        copy.wait()
 
 
 def local(sizes, leaf_up, parent_in, leaf_lists, parent_lists, up_transfer, down_transfer, check_inverse):
@@ -507,19 +516,20 @@
     constants = [jnp.asarray(tables()[name]) for name in names]
     operands = [leaf_up, parent_in, leaf_lists, parent_lists, up_transfer, down_transfer, check_inverse] + constants
     scratch = [pltpu.VMEM(x.shape, x.dtype) for x in operands]
-    scratch += [pltpu.VMEM((4, DENS, DENS), BF16)] * 2 + [pltpu.VMEM((DENS, DENS), BF16)] * 2
-
-    def sides(x_shape, strip):
+    scratch += [pltpu.VMEM((4, DENS, DENS), BF16)] * 2
+
+    def sides(x_shape, rows_here, total):
         return [
-            pltpu.VMEM((2, 2, strip, DENS), F32),
-            pltpu.VMEM((2, 2, 8, DENS), F32),
+            pltpu.VMEM((2, 2 * rows_here, DENS), F32),
+            pltpu.VMEM((2, 2, 4, DENS), F32),
             pltpu.VMEM((2, 2) + x_shape + (DENS,), F32),
-            pltpu.VMEM((2, 2, strip, DENS), F32),
-            pltpu.VMEM((2, 2, 8, DENS), F32),
-            pltpu.VMEM((4 * strip + 32, 512), F32),
+            pltpu.VMEM((2, 2 * rows_here, DENS), F32),
+            pltpu.VMEM((2, 2, 4, DENS), F32),
+            pltpu.VMEM((total, 512), F32),
         ]
 
-    scratch += sides((2, places), rows) + sides((pwidth,), 16)
+    scratch += sides((2, places), rows, 4 * width + 4 * rows + 16)
+    scratch += sides((pwidth,), prows, 4 * pwidth + 4 * prows + 16)
     scratch += [
         pltpu.VMEM((rows, 2, places, DENS), F32),
         pltpu.VMEM((2, half + 2, 2, 16 + places, 512), F32),
@@ -536,14 +546,16 @@
         pltpu.SemaphoreType.DMA((8,)),
         pltpu.SemaphoreType.DMA((8,)),
     ]
-    check, parent_up = pl.pallas_call(
+    check, parent_up, high, low = pl.pallas_call(
         functools.partial(near_body, sizes),
         out_shape=(
             pltpu.VMEM((rows, 2, places, DENS), F32),
             pltpu.VMEM((prows, pwidth, DENS), F32),
+            pltpu.VMEM((DENS, DENS), BF16),
+            pltpu.VMEM((DENS, DENS), BF16),
         ),
         in_specs=[pl.BlockSpec(memory_space=pltpu.HBM)] * len(operands),
-        out_specs=(pl.BlockSpec(memory_space=pltpu.VMEM),) * 2,
+        out_specs=(pl.BlockSpec(memory_space=pltpu.VMEM),) * 4,
         scratch_shapes=scratch,
         compiler_params=pltpu.CompilerParams(
             collective_id=0, has_side_effects=True, vmem_limit_bytes=60 * 1024 * 1024
@@ -555,10 +567,11 @@
             jax.ShapeDtypeStruct((rows, width, DENS), F32),
             jax.ShapeDtypeStruct((prows, pwidth, DENS), F32),
         ),
-        in_specs=[pl.BlockSpec(memory_space=pltpu.VMEM)] * 3,
-        out_specs=(pl.BlockSpec(memory_space=pltpu.VMEM),) * 2,
+        in_specs=[pl.BlockSpec(memory_space=pltpu.VMEM)] * 4,
+        out_specs=(pl.BlockSpec(memory_space=pltpu.HBM),) * 2,
+        scratch_shapes=[pltpu.VMEM((rows, width, DENS), F32), pltpu.SemaphoreType.DMA((3,))],
         compiler_params=pltpu.CompilerParams(vmem_limit_bytes=16 * 1024 * 1024),
-    )(check, parent_up, check_inverse)
+    )(check, parent_up, high, low)
 
 
 def solution(mesh):

time: 26.8 us -> 23.9 us (0.89)
  the two profiles are of different devices: /device:TPU:0 before, /device:TPU:1 now
where the time goes in v3:
time: 23.9 us; the launch traced here: 23.8 us
  Pallas kernels  23.1 us (97%)
  between operations  0.64 us (3%)
    pallas_call x1, Pallas kernels, local(): pl.pallas_call(functools.partial(near_body, sizes), out_shape=(pltpu.VMEM...  21 us
    pallas_call x1, Pallas kernels, local(): pl.pallas_call(last_body, out_shape=(jax.ShapeDtypeStruct((rows, width, D...  2.14 us

profile of v3, /device:TPU:1, one launch (start us, length us, event | category | flops | bytes accessed | tf_op | source)
XLA Modules:
  0.0 23.8 jit_solution(6621845563001755564)
XLA Ops:
  0.6 21.0 %shard_map.149 = (f32[24,2,8,456]{3,2,1,0:T(8,128)S(1)}, f32[12,8,456]{2,1,0:T(8,128)S(1)}, bf16[456,456]{1,0:T(8,128)(2,1)S(1)}, bf16[456,456]{1,0:T(8,128)(2,1)S(1)}) custom-call(f32[24,16,456]{2,1,0:T(8,128)} %leaf_hbm.1, f32[12,8,456]{2,1,0:T(8,128)} %parent_in_hbm.1, s32[24,16,40]{2,1,0:T(8,128)} %leaf_lists_hbm.1, s32[12,8,40]{2,1,0:T(8,128)} %parent_lists_hbm.1, ...), custom_call_target="tpu_custom_call" | custom-call | tf_op jit(solution)/shard_map/pallas_call | solution.py:549
  21.6 2.1 %shard_map.150 = (f32[24,16,456]{2,1,0:T(8,128)}, f32[12,8,456]{2,1,0:T(8,128)}) custom-call(f32[24,2,8,456]{3,2,1,0:T(8,128)S(1)} %get-tuple-element.6.check, f32[12,8,456]{2,1,0:T(8,128)S(1)} %get-tuple-element.7.parent_up, bf16[456,456]{1,0:T(8,128)(2,1)S(1)} %get-tuple-element.8.high, bf16[456,456]{1,0:T(8,128)(2,1)S(1)} %get-tuple-element.9.low), custom_call_target="tpu_custom_call" | custom-call | tf_op jit(solution)/shard_map/pallas_call | solution.py:564

commit v4 on v3

--- a/solution.py
+++ b/solution.py
@@ -181,7 +181,7 @@
     return jnp.where(lax.rem(lax.div(lane_index(shape), 128), 2) == 1, -1.0, 1.0)
 
 
-DIRECTIONS = [(-1, 0), (1, 0), (0, -1), (0, 1), (-1, -1), (-1, 1), (1, -1), (1, 1)]
+DIRECTIONS = [(0, -1), (0, 1), (-1, -1), (-1, 1), (1, -1), (1, 1), (-1, 0), (1, 0)]
 
 
 def pack_sides(row_of, strips, corners, rows, width):
@@ -227,6 +227,12 @@
     return copies
 
 
+def finish(copies, n):
+    dx, dy = DIRECTIONS[n]
+    copies[n].wait_send()
+    copies[DIRECTIONS.index((-dx, -dy))].wait_recv()
+
+
 def project_sides(held, got_x, got_y, got_c, doubled, special):
     parts = [got_x[...].reshape(-1, DENS), got_y[...].reshape(-1, DENS)]
     parts += [got_c[sx, sy] for sx in range(2) for sy in range(2)]
@@ -346,7 +352,7 @@
     return found
 
 
-def interact(levels, weights, total, group):
+def interact(levels, weights, total, group, between=()):
     for first in range(0, COUNT, group):
         last = min(first + group, COUNT)
         parts = [[], []]
@@ -372,6 +378,8 @@
                 total[:, cols] = term
             else:
                 total[:, cols] += term
+        if first // group < len(between):
+            between[first // group]()
 
 
 def near_body(
@@ -396,8 +404,18 @@
         (lax.rem(gx + dx + gx_size, gx_size), lax.rem(gy + dy + gy_size, gy_size)) for dx, dy in DIRECTIONS
     ]
     barrier = pltpu.get_barrier_semaphore()
-    for place in ids:
-        pl.semaphore_signal(barrier, inc=1, device_id=place, device_id_type=MESH)
+    inside = [
+        (gx + dx >= 0) & (gx + dx < gx_size) & (gy + dy >= 0) & (gy + dy < gy_size) for dx, dy in DIRECTIONS
+    ]
+    count = sum(here.astype(jnp.int32) for here in inside)
+
+    def each(action):
+        for n, here in enumerate(inside):
+            pl.when(here)(functools.partial(action, n))
+
+    for got in (leaf_got_x, leaf_got_y, leaf_got_c, parent_got_x, parent_got_y, parent_got_c):
+        got[...] = jnp.zeros_like(got)
+    each(lambda n: pl.semaphore_signal(barrier, inc=1, device_id=ids[n], device_id_type=MESH))
 
     pairs = [(leaf_hbm, leaf)]
     pairs += [(up_hbm.at[c], up.at[c]) for c in range(4)]
@@ -413,12 +431,11 @@
     for cy in range(2):
         children[:, cy] = leaf[...].reshape(rows, places, 2, DENS)[:, :, cy, :]
     pack_sides(lambda x, y: leaf[x, y : y + 1, :], leaf_strips, leaf_corners, rows, width)
-    pl.semaphore_wait(barrier, len(DIRECTIONS))
+    pl.semaphore_wait(barrier, count)
     leaf_copies = side_copies(
         children, leaf_strips, leaf_corners, leaf_got_x, leaf_got_y, leaf_got_c, leaf_send, leaf_recv, rows, ids
     )
-    for copy in leaf_copies:
-        copy.start()
+    each(lambda n: leaf_copies[n].start())
     for c in range(4):
         loads[1 + c].wait()
         child = children[...].reshape(prows, 2, 2, pwidth, DENS)[:, c // 2, c % 2].reshape(prows * pwidth, DENS)
@@ -432,8 +449,7 @@
         parent_up, parent_strips, parent_corners, parent_got_x, parent_got_y, parent_got_c,
         parent_send, parent_recv, prows, ids,
     )
-    for copy in parent_copies:
-        copy.start()
+    each(lambda n: parent_copies[n].start())
 
     for load in loads[5:13]:
         load.wait()
@@ -444,23 +460,25 @@
         leaf_marks[cx] = value
     for cx, value in enumerate(parent_flags(parent_lists, picks, prows, pwidth)):
         parent_marks[cx] = value
-    for c in range(4):
-        down_high[c], down_low[c] = split(down[c])
-    inverse_high[...], inverse_low[...] = split(inverse[...])
     for load in loads[13:]:
         load.wait()
-    for copy in leaf_copies:
-        copy.wait()
+    each(functools.partial(finish, leaf_copies))
     project_sides(leaf_held, leaf_got_x, leaf_got_y, leaf_got_c, *basis)
     fill_leaf_sides(leaf_padded, leaf_held, rows, places)
     shift_leaf(leaf_padded, leaf_shifted, sign_y, places)
-    for copy in parent_copies:
-        copy.wait()
+    each(functools.partial(finish, parent_copies))
     project_sides(parent_held, parent_got_x, parent_got_y, parent_got_c, *basis)
     fill_parent_sides(parent_padded, parent_held, prows, pwidth)
     shift_parent(parent_padded, parent_shifted, sign_y, pwidth)
     levels = [(leaf_shifted, leaf_marks, half, width), (parent_shifted, parent_marks, phalf, pwidth)]
-    interact(levels, weights, total, 3)
+
+    def split_down(c):
+        down_high[c], down_low[c] = split(down[c])
+
+    def split_inverse():
+        inverse_high[...], inverse_low[...] = split(inverse[...])
+
+    interact(levels, weights, total, 3, [functools.partial(split_down, c) for c in range(4)] + [split_inverse])
 
     signs = sign_y[0:1, :].reshape(1, 1, 512)
     leaf_count, parent_count = rows * width, prows * pwidth

time: 23.9 us -> 21 us (0.88)
  the two profiles are of different devices: /device:TPU:1 before, /device:TPU:7 now
where the time goes in v4:
time: 21 us; the launch traced here: 20.9 us
  Pallas kernels  20.3 us (97%)
  between operations  0.64 us (3%)
    pallas_call x1, Pallas kernels, local(): pl.pallas_call(functools.partial(near_body, sizes), out_shape=(pltpu.VMEM...  18.1 us
    pallas_call x1, Pallas kernels, local(): pl.pallas_call(last_body, out_shape=(jax.ShapeDtypeStruct((rows, width, D...  2.14 us

profile of v4, /device:TPU:7, one launch (start us, length us, event | category | flops | bytes accessed | tf_op | source)
XLA Modules:
  0.0 20.9 jit_solution(9222749684633823260)
XLA Ops:
  0.6 18.1 %shard_map.149 = (f32[24,2,8,456]{3,2,1,0:T(8,128)S(1)}, f32[12,8,456]{2,1,0:T(8,128)S(1)}, bf16[456,456]{1,0:T(8,128)(2,1)S(1)}, bf16[456,456]{1,0:T(8,128)(2,1)S(1)}) custom-call(f32[24,16,456]{2,1,0:T(8,128)} %leaf_hbm.1, f32[12,8,456]{2,1,0:T(8,128)} %parent_in_hbm.1, s32[24,16,40]{2,1,0:T(8,128)} %leaf_lists_hbm.1, s32[12,8,40]{2,1,0:T(8,128)} %parent_lists_hbm.1, ...), custom_call_target="tpu_custom_call" | custom-call | tf_op jit(solution)/shard_map/pallas_call | solution.py:567
  18.8 2.1 %shard_map.150 = (f32[24,16,456]{2,1,0:T(8,128)}, f32[12,8,456]{2,1,0:T(8,128)}) custom-call(f32[24,2,8,456]{3,2,1,0:T(8,128)S(1)} %get-tuple-element.6.check, f32[12,8,456]{2,1,0:T(8,128)S(1)} %get-tuple-element.7.parent_up, bf16[456,456]{1,0:T(8,128)(2,1)S(1)} %get-tuple-element.8.high, bf16[456,456]{1,0:T(8,128)(2,1)S(1)} %get-tuple-element.9.low), custom_call_target="tpu_custom_call" | custom-call | tf_op jit(solution)/shard_map/pallas_call | solution.py:582

commit v5 on v4

--- a/solution.py
+++ b/solution.py
@@ -18,7 +18,13 @@
 MESH = pl.DeviceIdType.MESH
 
 ALL_OFFSETS = [(a, b) for a in range(-3, 4) for b in range(-3, 4) if max(abs(a), abs(b)) >= 2]
-EVEN_OFFSETS = [(a, b) for a in range(-2, 4) for b in range(-2, 4) if max(abs(a), abs(b)) >= 2]
+EVEN_OFFSETS = [
+    (a, b)
+    for steps in ((-2, -1), (0, 1), (2, 3))
+    for a in range(-2, 4)
+    for b in steps
+    if max(abs(a), abs(b)) >= 2
+]
 COUNT = len(EVEN_OFFSETS)
 
 
@@ -233,10 +239,11 @@
     copies[DIRECTIONS.index((-dx, -dy))].wait_recv()
 
 
-def project_sides(held, got_x, got_y, got_c, doubled, special):
-    parts = [got_x[...].reshape(-1, DENS), got_y[...].reshape(-1, DENS)]
+def project_sides(got_x, got_y, got_c, doubled, special):
+    parts = [got_x[...].reshape(-1, DENS)] if got_x is not None else []
+    parts += [got_y[...].reshape(-1, DENS)]
     parts += [got_c[sx, sy] for sx in range(2) for sy in range(2)]
-    held[...] = project(jnp.concatenate(parts, axis=0), doubled, special)
+    return project(jnp.concatenate(parts, axis=0), doubled, special)
 
 
 def place_sides(put, held, first, rows):
@@ -262,24 +269,27 @@
             padded[parity, 1 + c : 1 + c + chunk, :, 8 : 8 + places, :] = value[:, parity]
 
 
-def fill_leaf_sides(padded, held, rows, places):
+def fill_leaf_x(padded, got_x, doubled, special, rows, places):
     half = rows // 2
-    value = held[0 : 8 * places, :].reshape(2, 2, 2, places, 512)
+    value = project(got_x[...].reshape(8 * places, DENS), doubled, special).reshape(2, 2, places, 2, 512)
     for side in range(2):
         for parity in range(2):
-            padded[parity, (half + 1) * side, :, 8 : 8 + places, :] = value[side, parity]
-
+            for cy in range(2):
+                padded[parity, (half + 1) * side, cy, 8 : 8 + places, :] = value[side, parity, :, cy]
+
+
+def fill_leaf_y(padded, held, rows, places):
     def put(parity, x, side, col, row):
         y = 8 + places if side else 7
         padded[parity, x, col, y : y + 1, :] = row
 
-    place_sides(put, held, 8 * places, rows)
-
-
-def shift_leaf(padded, shifted, sign_y, places):
+    place_sides(put, held, 0, rows)
+
+
+def shift_leaf(padded, shifted, sign_y, places, steps):
     signs = sign_y[0:1, :].reshape(1, 1, 512)
-    for d in range(6):
-        step = d - 2
+    for step in steps:
+        d = step + 2
         for parity in range(2):
             found = []
             for target in range(2):
@@ -352,34 +362,40 @@
     return found
 
 
-def interact(levels, weights, total, group, between=()):
-    for first in range(0, COUNT, group):
-        last = min(first + group, COUNT)
-        parts = [[], []]
-        for k in range(first, last):
-            a, b = EVEN_OFFSETS[k]
-            pieces = [[] for _ in range(4)]
-            for shifted, flags, half, width in levels:
-                for cx in range(2):
-                    source = cx + (-a if cx else a)
-                    parity, start = source % 2, source // 2 + 1
-                    flag = flags[cx, :, :, k : k + 1]
-                    flag = jnp.broadcast_to(flag, (half, width, 128)).astype(shifted.dtype)
-                    for t in range(4):
-                        mask = -flag if (cx and t % 2) else flag
-                        piece = shifted[b + 2, parity, start : start + half, :, lanes(t)] * mask
-                        pieces[t].append(piece.reshape(half * width, 128).astype(BF16))
-            for t in range(4):
-                parts[t // 2].append(jnp.concatenate(pieces[t], axis=0))
-        for z in range(2):
-            term = mm(jnp.concatenate(parts[z], axis=1), weights[z, first * 256 : last * 256, :])
-            cols = slice(256 * z, 256 * z + 256)
-            if first == 0:
-                total[:, cols] = term
+GROUPS = [tuple(range(first, first + 3)) for first in range(0, COUNT, 3)]
+
+
+def block_pieces(shifted, flags, half, width, k):
+    a, b = EVEN_OFFSETS[k]
+    pieces = [[] for _ in range(4)]
+    for cx in range(2):
+        source = cx + (-a if cx else a)
+        parity, start = source % 2, source // 2 + 1
+        flag = jnp.broadcast_to(flags[cx, :, :, k : k + 1], (half, width, 128)).astype(shifted.dtype)
+        for t in range(4):
+            mask = -flag if (cx and t % 2) else flag
+            piece = shifted[b + 2, parity, start : start + half, :, lanes(t)] * mask
+            pieces[t].append(piece.reshape(half * width, 128).astype(BF16))
+    return [jnp.concatenate(piece, axis=0) for piece in pieces]
+
+
+def interact(group, weights, levels):
+    parts = [[], []]
+    for k in group:
+        found = [level[0](k) for level in levels]
+        for t in range(4):
+            parts[t // 2].append(jnp.concatenate([one[t] for one in found], axis=0))
+    for z in range(2):
+        rows = slice(256 * group[0], 256 * group[-1] + 256)
+        term = mm(jnp.concatenate(parts[z], axis=1), weights[z, rows, :])
+        cols = slice(256 * z, 256 * z + 256)
+        at = 0
+        for _, count, total, first in levels:
+            if first:
+                total[:, cols] = term[at : at + count]
             else:
-                total[:, cols] += term
-        if first // group < len(between):
-            between[first // group]()
+                total[:, cols] += term[at : at + count]
+            at += count
 
 
 def near_body(
@@ -393,7 +409,7 @@
     leaf_strips, leaf_corners, leaf_got_x, leaf_got_y, leaf_got_c, leaf_held,
     parent_strips, parent_corners, parent_got_x, parent_got_y, parent_got_c, parent_held,
     children, leaf_padded, leaf_shifted, leaf_marks,
-    parent_padded, parent_shifted, parent_marks, parent_local, total,
+    parent_padded, parent_shifted, parent_marks, parent_local, leaf_total, parent_total,
     load_sem, leaf_send, leaf_recv, parent_send, parent_recv,
 ):
     rows, width, prows, pwidth, gx_size, gy_size = sizes
@@ -409,9 +425,9 @@
     ]
     count = sum(here.astype(jnp.int32) for here in inside)
 
-    def each(action):
-        for n, here in enumerate(inside):
-            pl.when(here)(functools.partial(action, n))
+    def each(action, first=0, last=len(DIRECTIONS)):
+        for n in range(first, last):
+            pl.when(inside[n])(functools.partial(action, n))
 
     for got in (leaf_got_x, leaf_got_y, leaf_got_c, parent_got_x, parent_got_y, parent_got_c):
         got[...] = jnp.zeros_like(got)
@@ -428,14 +444,14 @@
         load.start()
 
     loads[0].wait()
-    for cy in range(2):
-        children[:, cy] = leaf[...].reshape(rows, places, 2, DENS)[:, :, cy, :]
     pack_sides(lambda x, y: leaf[x, y : y + 1, :], leaf_strips, leaf_corners, rows, width)
     pl.semaphore_wait(barrier, count)
     leaf_copies = side_copies(
-        children, leaf_strips, leaf_corners, leaf_got_x, leaf_got_y, leaf_got_c, leaf_send, leaf_recv, rows, ids
+        leaf, leaf_strips, leaf_corners, leaf_got_x, leaf_got_y, leaf_got_c, leaf_send, leaf_recv, rows, ids
     )
     each(lambda n: leaf_copies[n].start())
+    for cy in range(2):
+        children[:, cy] = leaf[...].reshape(rows, places, 2, DENS)[:, :, cy, :]
     for c in range(4):
         loads[1 + c].wait()
         child = children[...].reshape(prows, 2, 2, pwidth, DENS)[:, c // 2, c % 2].reshape(prows * pwidth, DENS)
@@ -462,27 +478,35 @@
         parent_marks[cx] = value
     for load in loads[13:]:
         load.wait()
-    each(functools.partial(finish, leaf_copies))
-    project_sides(leaf_held, leaf_got_x, leaf_got_y, leaf_got_c, *basis)
-    fill_leaf_sides(leaf_padded, leaf_held, rows, places)
-    shift_leaf(leaf_padded, leaf_shifted, sign_y, places)
+    each(functools.partial(finish, leaf_copies), 6)
+    fill_leaf_x(leaf_padded, leaf_got_x, *basis, rows, places)
+    shift_leaf(leaf_padded, leaf_shifted, sign_y, places, (0, 1))
+    leaf_pieces = functools.partial(block_pieces, leaf_shifted, leaf_marks, half, width)
+    for group in GROUPS[3:5]:
+        interact(group, weights, [(leaf_pieces, rows * width, leaf_total, group == GROUPS[3])])
+
+    each(functools.partial(finish, leaf_copies), 0, 6)
+    leaf_held[...] = project_sides(None, leaf_got_y, leaf_got_c, *basis)
+    fill_leaf_y(leaf_padded, leaf_held, rows, places)
+    shift_leaf(leaf_padded, leaf_shifted, sign_y, places, (-2, -1, 2, 3))
     each(functools.partial(finish, parent_copies))
-    project_sides(parent_held, parent_got_x, parent_got_y, parent_got_c, *basis)
+    parent_held[...] = project_sides(parent_got_x, parent_got_y, parent_got_c, *basis)
     fill_parent_sides(parent_padded, parent_held, prows, pwidth)
     shift_parent(parent_padded, parent_shifted, sign_y, pwidth)
-    levels = [(leaf_shifted, leaf_marks, half, width), (parent_shifted, parent_marks, phalf, pwidth)]
-
-    def split_down(c):
-        down_high[c], down_low[c] = split(down[c])
-
-    def split_inverse():
-        inverse_high[...], inverse_low[...] = split(inverse[...])
-
-    interact(levels, weights, total, 3, [functools.partial(split_down, c) for c in range(4)] + [split_inverse])
+    parent_pieces = functools.partial(block_pieces, parent_shifted, parent_marks, phalf, pwidth)
+    for turn, group in enumerate(GROUPS[:3] + GROUPS[5:]):
+        levels = [(leaf_pieces, rows * width, leaf_total, False)]
+        interact(group, weights, levels + [(parent_pieces, prows * pwidth, parent_total, turn == 0)])
+        if turn < 4:
+            down_high[turn], down_low[turn] = split(down[turn])
+        elif turn == 4:
+            inverse_high[...], inverse_low[...] = split(inverse[...])
+    for group in GROUPS[3:5]:
+        interact(group, weights, [(parent_pieces, prows * pwidth, parent_total, False)])
 
     signs = sign_y[0:1, :].reshape(1, 1, 512)
     leaf_count, parent_count = rows * width, prows * pwidth
-    y = total[leaf_count : leaf_count + parent_count, :].reshape(2, phalf, pwidth, 512)
+    y = parent_total[...].reshape(2, phalf, pwidth, 512)
     row = lax.broadcasted_iota(jnp.int32, (phalf, pwidth, 512), 1)
     y = [jnp.where(lax.rem(row, 2) == 0, part, part * signs) for part in (y[0], y[1] * turned((1, 1, 512)))]
     y = jnp.concatenate(y, axis=0).reshape(parent_count, 512)
@@ -494,7 +518,7 @@
 
     quarter = leaf_count // 4
     for c in range(4):
-        y = total[c * quarter : (c + 1) * quarter, :].reshape(half // 2, 2, places, 512)
+        y = leaf_total[c * quarter : (c + 1) * quarter, :].reshape(half // 2, 2, places, 512)
         if c >= 2:
             y = y * turned((1, 1, 1, 512))
         y = jnp.concatenate([y[:, 0:1], y[:, 1:2] * signs.reshape(1, 1, 1, 512)], axis=1).reshape(quarter, 512)
@@ -546,7 +570,7 @@
             pltpu.VMEM((total, 512), F32),
         ]
 
-    scratch += sides((2, places), rows, 4 * width + 4 * rows + 16)
+    scratch += sides((width,), rows, 4 * rows + 16)
     scratch += sides((pwidth,), prows, 4 * pwidth + 4 * prows + 16)
     scratch += [
         pltpu.VMEM((rows, 2, places, DENS), F32),
@@ -557,7 +581,8 @@
         pltpu.VMEM((6, 2, phalf + 2, pwidth, 512), F32),
         pltpu.VMEM((2, phalf, pwidth, 128), F32),
         pltpu.VMEM((prows, pwidth, DENS), F32),
-        pltpu.VMEM((rows * width + prows * pwidth, 512), F32),
+        pltpu.VMEM((rows * width, 512), F32),
+        pltpu.VMEM((prows * pwidth, 512), F32),
         pltpu.SemaphoreType.DMA((17,)),
         pltpu.SemaphoreType.DMA((8,)),
         pltpu.SemaphoreType.DMA((8,)),

time: 21 us -> 20.1 us (0.957); the launches traced: 20.9 us -> 19.8 us
  Pallas kernels: 20.3 us -> 19.2 us
    pallas_call x1, Pallas kernels: 18.1 us -> 17 us  [local(): pl.pallas_call(functools.partial(near_body, sizes), out_shape=(pltpu.VMEM...]
where the time goes in v5:
time: 20.1 us; the launch traced here: 19.8 us
  Pallas kernels  19.2 us (96%)
  between operations  0.64 us (3%)
    pallas_call x1, Pallas kernels, local(): pl.pallas_call(functools.partial(near_body, sizes), out_shape=(pltpu.VMEM...  17 us
    pallas_call x1, Pallas kernels, local(): pl.pallas_call(last_body, out_shape=(jax.ShapeDtypeStruct((rows, width, D...  2.14 us

profile of v5, /device:TPU:7, one launch (start us, length us, event | category | flops | bytes accessed | tf_op | source)
XLA Modules:
  0.0 19.8 jit_solution(14686508076537341368)
XLA Ops:
  0.6 17.0 %shard_map.149 = (f32[24,2,8,456]{3,2,1,0:T(8,128)S(1)}, f32[12,8,456]{2,1,0:T(8,128)S(1)}, bf16[456,456]{1,0:T(8,128)(2,1)S(1)}, bf16[456,456]{1,0:T(8,128)(2,1)S(1)}) custom-call(f32[24,16,456]{2,1,0:T(8,128)} %leaf_hbm.1, f32[12,8,456]{2,1,0:T(8,128)} %parent_in_hbm.1, s32[24,16,40]{2,1,0:T(8,128)} %leaf_lists_hbm.1, s32[12,8,40]{2,1,0:T(8,128)} %parent_lists_hbm.1, ...), custom_call_target="tpu_custom_call" | custom-call | tf_op jit(solution)/shard_map/pallas_call | solution.py:592
  17.7 2.1 %shard_map.150 = (f32[24,16,456]{2,1,0:T(8,128)}, f32[12,8,456]{2,1,0:T(8,128)}) custom-call(f32[24,2,8,456]{3,2,1,0:T(8,128)S(1)} %get-tuple-element.6.check, f32[12,8,456]{2,1,0:T(8,128)S(1)} %get-tuple-element.7.parent_up, bf16[456,456]{1,0:T(8,128)(2,1)S(1)} %get-tuple-element.8.high, bf16[456,456]{1,0:T(8,128)(2,1)S(1)} %get-tuple-element.9.low), custom_call_target="tpu_custom_call" | custom-call | tf_op jit(solution)/shard_map/pallas_call | solution.py:607

commit v6 on v5

--- a/solution.py
+++ b/solution.py
@@ -189,6 +189,8 @@
 
 DIRECTIONS = [(0, -1), (0, 1), (-1, -1), (-1, 1), (1, -1), (1, 1), (-1, 0), (1, 0)]
 
+SENDS = (2, 3, 4, 5, 0, 1, 6, 7)
+
 
 def pack_sides(row_of, strips, corners, rows, width):
     half = rows // 2
@@ -415,6 +417,16 @@
     rows, width, prows, pwidth, gx_size, gy_size = sizes
     half, phalf = rows // 2, prows // 2
     places = width // 2
+    pairs = [(leaf_hbm, leaf)]
+    pairs += [(up_hbm.at[c], up.at[c]) for c in range(4)]
+    pairs += [(doubled_hbm, doubled), (special_hbm, special), (sign_hbm, sign_y), (picks_hbm, picks)]
+    pairs += [(leaf_lists_hbm, leaf_lists), (parent_lists_hbm, parent_lists)]
+    pairs += [(down_hbm, down), (inverse_hbm, inverse), (weights_hbm, weights)]
+    pairs += [(doubled_t_hbm, doubled_t), (special_t_hbm, special_t), (parent_in_hbm, parent_in)]
+    loads = [pltpu.make_async_copy(a, b, load_sem.at[n]) for n, (a, b) in enumerate(pairs)]
+    for load in loads:
+        load.start()
+
     gx, gy = lax.axis_index("gx"), lax.axis_index("gy")
     ids = [
         (lax.rem(gx + dx + gx_size, gx_size), lax.rem(gy + dy + gy_size, gy_size)) for dx, dy in DIRECTIONS
@@ -425,23 +437,13 @@
     ]
     count = sum(here.astype(jnp.int32) for here in inside)
 
-    def each(action, first=0, last=len(DIRECTIONS)):
-        for n in range(first, last):
+    def each(action, turns=tuple(range(len(DIRECTIONS)))):
+        for n in turns:
             pl.when(inside[n])(functools.partial(action, n))
 
     for got in (leaf_got_x, leaf_got_y, leaf_got_c, parent_got_x, parent_got_y, parent_got_c):
         got[...] = jnp.zeros_like(got)
     each(lambda n: pl.semaphore_signal(barrier, inc=1, device_id=ids[n], device_id_type=MESH))
-
-    pairs = [(leaf_hbm, leaf)]
-    pairs += [(up_hbm.at[c], up.at[c]) for c in range(4)]
-    pairs += [(doubled_hbm, doubled), (special_hbm, special), (sign_hbm, sign_y), (picks_hbm, picks)]
-    pairs += [(leaf_lists_hbm, leaf_lists), (parent_lists_hbm, parent_lists)]
-    pairs += [(down_hbm, down), (inverse_hbm, inverse), (weights_hbm, weights)]
-    pairs += [(doubled_t_hbm, doubled_t), (special_t_hbm, special_t), (parent_in_hbm, parent_in)]
-    loads = [pltpu.make_async_copy(a, b, load_sem.at[n]) for n, (a, b) in enumerate(pairs)]
-    for load in loads:
-        load.start()
 
     loads[0].wait()
     pack_sides(lambda x, y: leaf[x, y : y + 1, :], leaf_strips, leaf_corners, rows, width)
@@ -449,7 +451,7 @@
     leaf_copies = side_copies(
         leaf, leaf_strips, leaf_corners, leaf_got_x, leaf_got_y, leaf_got_c, leaf_send, leaf_recv, rows, ids
     )
-    each(lambda n: leaf_copies[n].start())
+    each(lambda n: leaf_copies[n].start(), SENDS)
     for cy in range(2):
         children[:, cy] = leaf[...].reshape(rows, places, 2, DENS)[:, :, cy, :]
     for c in range(4):
@@ -465,7 +467,7 @@
         parent_up, parent_strips, parent_corners, parent_got_x, parent_got_y, parent_got_c,
         parent_send, parent_recv, prows, ids,
     )
-    each(lambda n: parent_copies[n].start())
+    each(lambda n: parent_copies[n].start(), SENDS)
 
     for load in loads[5:13]:
         load.wait()
@@ -478,14 +480,14 @@
         parent_marks[cx] = value
     for load in loads[13:]:
         load.wait()
-    each(functools.partial(finish, leaf_copies), 6)
+    each(functools.partial(finish, leaf_copies), (6, 7))
     fill_leaf_x(leaf_padded, leaf_got_x, *basis, rows, places)
     shift_leaf(leaf_padded, leaf_shifted, sign_y, places, (0, 1))
     leaf_pieces = functools.partial(block_pieces, leaf_shifted, leaf_marks, half, width)
     for group in GROUPS[3:5]:
         interact(group, weights, [(leaf_pieces, rows * width, leaf_total, group == GROUPS[3])])
 
-    each(functools.partial(finish, leaf_copies), 0, 6)
+    each(functools.partial(finish, leaf_copies), tuple(range(6)))
     leaf_held[...] = project_sides(None, leaf_got_y, leaf_got_c, *basis)
     fill_leaf_y(leaf_padded, leaf_held, rows, places)
     shift_leaf(leaf_padded, leaf_shifted, sign_y, places, (-2, -1, 2, 3))

time: 20.1 us -> 19.2 us (0.955)
  Pallas kernels: 19.2 us -> 18.4 us
    pallas_call x1, Pallas kernels: 17 us -> 16.3 us  [local(): pl.pallas_call(functools.partial(near_body, sizes), out_shape=(pltpu.VMEM...]
where the time goes in v6:
time: 19.2 us; the launch traced here: 19.1 us
  Pallas kernels  18.4 us (96%)
  between operations  0.64 us (3%)
    pallas_call x1, Pallas kernels, local(): pl.pallas_call(functools.partial(near_body, sizes), out_shape=(pltpu.VMEM...  16.3 us
    pallas_call x1, Pallas kernels, local(): pl.pallas_call(last_body, out_shape=(jax.ShapeDtypeStruct((rows, width, D...  2.14 us

profile of v6, /device:TPU:7, one launch (start us, length us, event | category | flops | bytes accessed | tf_op | source)
XLA Modules:
  0.0 19.1 jit_solution(10747587617708325297)
XLA Ops:
  0.6 16.3 %shard_map.149 = (f32[24,2,8,456]{3,2,1,0:T(8,128)S(1)}, f32[12,8,456]{2,1,0:T(8,128)S(1)}, bf16[456,456]{1,0:T(8,128)(2,1)S(1)}, bf16[456,456]{1,0:T(8,128)(2,1)S(1)}) custom-call(f32[24,16,456]{2,1,0:T(8,128)} %leaf_hbm.1, f32[12,8,456]{2,1,0:T(8,128)} %parent_in_hbm.1, s32[24,16,40]{2,1,0:T(8,128)} %leaf_lists_hbm.1, s32[12,8,40]{2,1,0:T(8,128)} %parent_lists_hbm.1, ...), custom_call_target="tpu_custom_call" | custom-call | tf_op jit(solution)/shard_map/pallas_call | solution.py:594
  16.9 2.1 %shard_map.150 = (f32[24,16,456]{2,1,0:T(8,128)}, f32[12,8,456]{2,1,0:T(8,128)}) custom-call(f32[24,2,8,456]{3,2,1,0:T(8,128)S(1)} %get-tuple-element.6.check, f32[12,8,456]{2,1,0:T(8,128)S(1)} %get-tuple-element.7.parent_up, bf16[456,456]{1,0:T(8,128)(2,1)S(1)} %get-tuple-element.8.high, bf16[456,456]{1,0:T(8,128)(2,1)S(1)} %get-tuple-element.9.low), custom_call_target="tpu_custom_call" | custom-call | tf_op jit(solution)/shard_map/pallas_call | solution.py:609

commit v7 on v6

--- a/solution.py
+++ b/solution.py
@@ -486,6 +486,9 @@
     leaf_pieces = functools.partial(block_pieces, leaf_shifted, leaf_marks, half, width)
     for group in GROUPS[3:5]:
         interact(group, weights, [(leaf_pieces, rows * width, leaf_total, group == GROUPS[3])])
+    for c in range(4):
+        down_high[c], down_low[c] = split(down[c])
+    inverse_high[...], inverse_low[...] = split(inverse[...])
 
     each(functools.partial(finish, leaf_copies), tuple(range(6)))
     leaf_held[...] = project_sides(None, leaf_got_y, leaf_got_c, *basis)
@@ -499,10 +502,6 @@
     for turn, group in enumerate(GROUPS[:3] + GROUPS[5:]):
         levels = [(leaf_pieces, rows * width, leaf_total, False)]
         interact(group, weights, levels + [(parent_pieces, prows * pwidth, parent_total, turn == 0)])
-        if turn < 4:
-            down_high[turn], down_low[turn] = split(down[turn])
-        elif turn == 4:
-            inverse_high[...], inverse_low[...] = split(inverse[...])
     for group in GROUPS[3:5]:
         interact(group, weights, [(parent_pieces, prows * pwidth, parent_total, False)])
 

time: 19.2 us -> 20.1 us (1.047)
  Pallas kernels: 18.4 us -> 19.4 us
    pallas_call x1, Pallas kernels: 16.3 us -> 17.3 us  [local(): pl.pallas_call(functools.partial(near_body, sizes), out_shape=(pltpu.VMEM...]
where the time goes in v7:
time: 20.1 us; the launch traced here: 20 us
  Pallas kernels  19.4 us (97%)
  between operations  0.64 us (3%)
    pallas_call x1, Pallas kernels, local(): pl.pallas_call(functools.partial(near_body, sizes), out_shape=(pltpu.VMEM...  17.3 us
    pallas_call x1, Pallas kernels, local(): pl.pallas_call(last_body, out_shape=(jax.ShapeDtypeStruct((rows, width, D...  2.14 us

profile of v7, /device:TPU:7, one launch (start us, length us, event | category | flops | bytes accessed | tf_op | source)
XLA Modules:
  0.0 20.0 jit_solution(15390738175946095781)
XLA Ops:
  0.6 17.3 %shard_map.149 = (f32[24,2,8,456]{3,2,1,0:T(8,128)S(1)}, f32[12,8,456]{2,1,0:T(8,128)S(1)}, bf16[456,456]{1,0:T(8,128)(2,1)S(1)}, bf16[456,456]{1,0:T(8,128)(2,1)S(1)}) custom-call(f32[24,16,456]{2,1,0:T(8,128)} %leaf_hbm.1, f32[12,8,456]{2,1,0:T(8,128)} %parent_in_hbm.1, s32[24,16,40]{2,1,0:T(8,128)} %leaf_lists_hbm.1, s32[12,8,40]{2,1,0:T(8,128)} %parent_lists_hbm.1, ...), custom_call_target="tpu_custom_call" | custom-call | tf_op jit(solution)/shard_map/pallas_call | solution.py:593
  17.9 2.1 %shard_map.150 = (f32[24,16,456]{2,1,0:T(8,128)}, f32[12,8,456]{2,1,0:T(8,128)}) custom-call(f32[24,2,8,456]{3,2,1,0:T(8,128)S(1)} %get-tuple-element.6.check, f32[12,8,456]{2,1,0:T(8,128)S(1)} %get-tuple-element.7.parent_up, bf16[456,456]{1,0:T(8,128)(2,1)S(1)} %get-tuple-element.8.high, bf16[456,456]{1,0:T(8,128)(2,1)S(1)} %get-tuple-element.9.low), custom_call_target="tpu_custom_call" | custom-call | tf_op jit(solution)/shard_map/pallas_call | solution.py:608
